TPU v7x, 128 devices: a whole 4x4x4 slice. The times are simulated.
128 devices in a mesh: group: 4 (over y_lo, core), blk: 32 (over y_hi, x, z).
Axes of the slice: x: 4, y: 4 (y_hi: 2, y_lo: 2; y = y_hi * 2 + y_lo), z: 4, core: 2. Of those that a mesh axis runs over, the one named last changes fastest.
Arguments:
- embeddings: float32 [49152, 1024], P(('group', 'blk'))
- ranks: int32 [49152], P(('group', 'blk')), may hold values from 0 to 49151, each once
- routes: int32 [49152, 1], P(('group', 'blk')), may hold values from 0 to 127; in each aligned block of 384 rows (0 to 383, 384 to 767, ...) at most 6 rows name the same one
Outputs:
- earlier_max: float32 [49152], P(('group', 'blk'))
- later_max: float32 [49152], P(('group', 'blk'))
Inputs may be any that keep to these rules, and one draw needn't show every extreme that they name: `routes`: among the 384 documents of one source shard at most 6 name the same member block; some shard's documents name some block exactly 6 times.
All inputs are finite; a program needn't handle non-finite values.
Results may differ from a plain program's by a relative error of at most 0.0003.
Values may be sent and summed in bfloat16 or wider, within the bound.
A program may use at most 64 MiB of HBM per device.

v0:
```python
import jax
import jax.numpy as jnp
from jax import lax
from jax.sharding import PartitionSpec as P

STEPS = 4


def passed_along(block, axis, distance):
    devices = range(lax.axis_size(axis))
    route = [((i - distance) % len(devices), i) for i in devices]
    return lax.ppermute(block, axis, route)


def compare(left, left_rank, right, right_rank):
    scores = lax.dot_general(
        left, right, (((1,), (1,)), ((), ())), preferred_element_type=jnp.float32
    )
    valid = (left_rank[:, None] >= 0) & (right_rank[None, :] >= 0)
    lower = valid & (right_rank[None, :] < left_rank[:, None])
    higher = valid & (right_rank[None, :] > left_rank[:, None])
    low_scores = jnp.where(lower, scores, -1.0)
    high_scores = jnp.where(higher, scores, -1.0)
    return (low_scores.max(1), high_scores.max(1), high_scores.max(0), low_scores.max(0))


def body(embeddings, ranks, routes):
    row_count, feat_width = embeddings.shape
    groups_here = lax.axis_size("group")
    blocks_here = lax.axis_size("blk")
    total_devs = groups_here * blocks_here
    slot_count = 2 * row_count
    capacity = slot_count // total_devs
    mean_square = jnp.mean(embeddings * embeddings, axis=-1, keepdims=True)
    unit = (embeddings * lax.rsqrt(mean_square + 1e-06) * feat_width ** (-0.5)).astype(jnp.bfloat16)
    target = routes[:, 0]
    one_hot = (target[:, None] == jnp.arange(total_devs, dtype=jnp.int32)[None, :]).astype(
        jnp.int32
    )
    earlier_count = jnp.cumsum(one_hot, axis=0) - one_hot
    slot_index = jnp.sum(earlier_count * one_hot, axis=1)
    position = target * capacity + slot_index
    send_rows = jnp.zeros((total_devs * capacity, feat_width), jnp.bfloat16).at[position].set(unit)
    send_ranks = (
        jnp.full((total_devs * capacity,), -1, jnp.int32)
        .at[position]
        .set(ranks)
        .reshape(total_devs, capacity)
    )
    members = lax.all_to_all(
        send_rows.reshape(total_devs, capacity, feat_width),
        ("group", "blk"),
        split_axis=0,
        concat_axis=0,
        tiled=True,
    ).reshape(slot_count, feat_width)
    member_rank = lax.all_to_all(
        send_ranks, ("group", "blk"), split_axis=0, concat_axis=0, tiled=True
    ).reshape(slot_count)
    mine_early, mine_late, unused_early, unused_late = compare(
        members, member_rank, members, member_rank
    )
    ahead_rows, ahead_rank = (members, member_rank)
    behind_rows, behind_rank = (members, member_rank)
    for step_index in range(STEPS):
        ahead_rows = passed_along(ahead_rows, "blk", 1)
        ahead_rank = passed_along(ahead_rank, "blk", 1)
        behind_rows = passed_along(behind_rows, "blk", -1)
        behind_rank = passed_along(behind_rank, "blk", -1)
        left_early, left_late, unused_early, unused_late = compare(
            members, member_rank, ahead_rows, ahead_rank
        )
        mine_early = jnp.maximum(mine_early, left_early)
        mine_late = jnp.maximum(mine_late, left_late)
        left_early, left_late, unused_early, unused_late = compare(
            members, member_rank, behind_rows, behind_rank
        )
        mine_early = jnp.maximum(mine_early, left_early)
        mine_late = jnp.maximum(mine_late, left_late)
    results = jnp.stack([mine_early, mine_late]).reshape(2, total_devs, capacity)
    answers = lax.all_to_all(
        results, ("group", "blk"), split_axis=1, concat_axis=1, tiled=True
    ).reshape(2, total_devs * capacity)
    picked = answers[:, position]
    return (picked[0], picked[1])


def solution(mesh):
    placed = (P(("group", "blk"), None), P(("group", "blk")), P(("group", "blk"), None))
    return jax.shard_map(
        body,
        mesh=mesh,
        in_specs=placed,
        out_specs=(P(("group", "blk")), P(("group", "blk"))),
        check_vma=False,
    )
```

profile of v0, /device:TPU:1, one launch (start us, length us, event | category | flops | bytes accessed | tf_op | source)
XLA Modules:
  0.0 273.6 jit_solution(7830365563560873163)
XLA Ops:
  0.6 0.8 reduce
  1.5 0.1 copy.17
  1.6 0.2 fusion.4
  1.8 0.1 broadcast_add_fusion
  1.9 0.2 fusion.7
  2.2 0.2 multiply_reduce_fusion
  2.4 3.5 %scatter_custom_fusion.1 = bf16[768,1024]{1,0:T(8,128)(2,1)} fusion(s32[384]{0:T(512)S(1)} %fusion.11, f32[384,1024]{1,0:T(8,128)S(1)} %copy-done, f32[]{:T(128)} %constant.8.clone.1, f32[384]{0:T(512)S(1)} %add_rsqrt_fusion, bf16[]{:T(256)} %constant.4.clone.1), kind=kCustom, calls=%fused_computation.41 | custom fusion | flops 1179648 | bytes 3147782 | tf_op jit(solution)/shard_map/scatter | solution.py:43
  5.9 2.5 reshape.292
  8.4 40.5 %all_to_all.19 = bf16[128,6,1024]{2,1,0:T(8,128)(2,1)} all-to-all(bf16[128,6,1024]{2,1,0:T(8,128)(2,1)S(1)} %reshape.292), channel_id=1, replica_groups=mesh['group'=4,'blk'=32] {'group','blk'}, dimensions={0} | all-to-all | bytes 3145728 | tf_op jit(solution)/shard_map/all_to_all | solution.py:50
  48.8 2.6 reshape.293
  51.4 3.5 %collective-permute-start.3 = (bf16[768,1024]{1,0:T(8,128)(2,1)S(1)}, bf16[768,1024]{1,0:T(8,128)(2,1)}, u32[]{:S(2)}, u32[]{:S(2)}) collective-permute-start(bf16[768,1024]{1,0:T(8,128)(2,1)S(1)} %reshape.293), channel_id=1, source_target_pairs={{1,0},{2,1},{3,2},{4,3},{5,4},{6,5},{7,6},{8,7},{9,8},{10,9},{11,1... | collective-permute-start | bytes 4718600 | tf_op jit(solution)/shard_map/ppermute | solution.py:12
  55.0 0.0 collective-permute-start.1
  55.0 3.1 %scatter_custom_fusion = s32[768]{0:T(1024)S(1)} fusion(s32[384]{0:T(512)S(1)} %fusion.11, s32[384]{0:T(512)} %param.4, s32[]{:T(128)} %constant.11.clone.1), kind=kCustom, calls=%fused_computation.72 | custom fusion | bytes 3584 | tf_op jit(solution)/shard_map/scatter | solution.py:47
  58.0 0.1 all_to_all.12
  58.2 39.9 %all_to_all.20 = s32[128,1,6]{2,1,0:T(1,128)S(1)} all-to-all(s32[128,1,6]{2,1,0:T(1,128)S(1)} %bitcast.33), channel_id=1, replica_groups=mesh['group'=4,'blk'=32] {'group','blk'}, dimensions={0} | all-to-all | bytes 6144 | tf_op jit(solution)/shard_map/all_to_all | solution.py:57
  98.0 0.5 broadcast.102
  98.6 0.8 reduce.11
  99.4 0.1 broadcast_in_dim_reshape.2
  99.5 0.2 collective-permute-start.2
  99.7 1.3 collective-permute-start
  101.0 6.8 %collective-permute-done = s32[768]{0:T(1024)S(1)} collective-permute-done((s32[768]{0:T(1024)S(1)}, s32[768]{0:T(1024)S(1)}, u32[]{:S(2)}, u32[]{:S(2)}) %collective-permute-start) | collective-permute-done | bytes 3104 | tf_op jit(solution)/shard_map/ppermute | solution.py:12
  107.9 0.0 collective-permute-start.4
  107.9 0.0 collective-permute-done.3
  107.9 7.2 %collective-permute-start.7 = (bf16[768,1024]{1,0:T(8,128)(2,1)}, bf16[768,1024]{1,0:T(8,128)(2,1)S(1)}, u32[]{:S(2)}, u32[]{:S(2)}) collective-permute-start(bf16[768,1024]{1,0:T(8,128)(2,1)} %collective-permute-done.3), channel_id=1, source_target_pairs={{1,0},{2,1},{3,2},{4,3},{5,4},{6,5},{7,6},{8,7},{9,8},{10,9},{11,1... | collective-permute-start | bytes 4718600 | tf_op jit(solution)/shard_map/ppermute | solution.py:12
  115.1 0.0 collective-permute-done.2
  115.1 0.1 collective-permute-start.6
  115.2 0.9 collective-permute-done.4
  116.1 0.6 collective-permute-start.8
  116.7 0.0 collective-permute-done.1
  116.7 0.1 collective-permute-start.5
  116.8 30.2 %collective-permute-done.6 = s32[768]{0:T(1024)S(1)} collective-permute-done((s32[768]{0:T(1024)S(1)}, s32[768]{0:T(1024)S(1)}, u32[]{:S(2)}, u32[]{:S(2)}) %collective-permute-start.6) | collective-permute-done | bytes 3104 | tf_op jit(solution)/shard_map/ppermute | solution.py:12
  147.0 7.9 %collective-permute-start.10 = (s32[768]{0:T(1024)S(1)}, s32[768]{0:T(1024)S(1)}, u32[]{:S(2)}, u32[]{:S(2)}) collective-permute-start(s32[768]{0:T(1024)S(1)} %collective-permute-done.6), channel_id=1, source_target_pairs={{1,0},{2,1},{3,2},{4,3},{5,4},{6,5},{7,6},{8,7},{9,8},{10,9},{11,1... | collective-permute-start | bytes 9224 | tf_op jit(solution)/shard_map/ppermute | solution.py:12
  154.9 0.1 collective-permute-start.12
  155.0 0.7 collective-permute-done.10
  155.6 7.4 %collective-permute-start.14 = (s32[768]{0:T(1024)S(1)}, s32[768]{0:T(1024)S(1)}, u32[]{:S(2)}, u32[]{:S(2)}) collective-permute-start(s32[768]{0:T(1024)S(1)} %collective-permute-done.10), channel_id=1, source_target_pairs={{1,0},{2,1},{3,2},{4,3},{5,4},{6,5},{7,6},{8,7},{9,8},{10,9},{11,1... | collective-permute-start | bytes 9224 | tf_op jit(solution)/shard_map/ppermute | solution.py:12
  163.1 0.1 collective-permute-done.12
  163.2 0.7 collective-permute-done.14
  163.8 0.0 collective-permute-done.7
  163.8 7.7 %collective-permute-start.11 = (bf16[768,1024]{1,0:T(8,128)(2,1)S(1)}, bf16[768,1024]{1,0:T(8,128)(2,1)S(1)}, u32[]{:S(2)}, u32[]{:S(2)}) collective-permute-start(bf16[768,1024]{1,0:T(8,128)(2,1)S(1)} %collective-permute-done.7), channel_id=1, source_target_pairs={{1,0},{2,1},{3,2},{4,3},{5,4},{6,5},{7,6},{8,7},{9,8},{10,9},{11,1... | collective-permute-start | bytes 4718600 | tf_op jit(solution)/shard_map/ppermute | solution.py:12
  171.5 1.4 fusion.12
  172.9 0.1 collective-permute-start.9
  173.0 2.8 %fusion.13 = f32[768,768]{0,1:T(8,128)S(1)} fusion(bf16[768,1024]{1,0:T(8,128)(2,1)S(1)} %reshape.293, bf16[768,1024]{1,0:T(8,128)(2,1)} %collective-permute-done.1), kind=kOutput, calls=%fused_computation.76 | convolution fusion | flops 1207959552 | bytes 5505024 | tf_op jit(solution)/shard_map/dot_general | solution.py:16
  175.9 2.8 %fusion.14 = f32[768,768]{0,1:T(8,128)S(1)} fusion(bf16[768,1024]{1,0:T(8,128)(2,1)S(1)} %reshape.293, bf16[768,1024]{1,0:T(8,128)(2,1)} %collective-permute-done.3), kind=kOutput, calls=%fused_computation.77 | convolution fusion | flops 1207959552 | bytes 5505024 | tf_op jit(solution)/shard_map/dot_general | solution.py:16
  178.7 1.4 fusion.15
  180.1 1.4 fusion.16
  181.6 18.3 %collective-permute-done.11 = bf16[768,1024]{1,0:T(8,128)(2,1)S(1)} collective-permute-done((bf16[768,1024]{1,0:T(8,128)(2,1)S(1)}, bf16[768,1024]{1,0:T(8,128)(2,1)S(1)}, u32[]{:S(2)}, u32[]{:S(2)}) %collective-permute-start.11) | collective-permute-done | bytes 1572896 | tf_op jit(solution)/shard_map/ppermute | solution.py:12
  199.9 7.9 %collective-permute-start.15 = (bf16[768,1024]{1,0:T(8,128)(2,1)S(1)}, bf16[768,1024]{1,0:T(8,128)(2,1)S(1)}, u32[]{:S(2)}, u32[]{:S(2)}) collective-permute-start(bf16[768,1024]{1,0:T(8,128)(2,1)S(1)} %collective-permute-done.11), channel_id=1, source_target_pairs={{1,0},{2,1},{3,2},{4,3},{5,4},{6,5},{7,6},{8,7},{9,8},{10,9},{11,1... | collective-permute-start | bytes 4718600 | tf_op jit(solution)/shard_map/ppermute | solution.py:12
  207.8 1.4 fusion.17
  209.2 0.0 collective-permute-done.9
  209.2 0.1 collective-permute-start.13
  209.3 8.2 %select_reduce_fusion.16 = (f32[768]{0:T(1024)S(1)}, f32[768]{0:T(1024)S(1)}, f32[768]{0:T(1024)S(1)}, f32[768]{0:T(1024)S(1)}, f32[768]{0:T(1024)S(1)}, /*index...) fusion(f32[768,768]{0,1:T(8,128)S(1)} %fusion.13, ...), kind=kOutput, calls=%fused_computation.37 | convolution fusion | flops 1239800832 | bytes 15002112 | tf_op jit(solution)/shard_map/dot_general | solution.py:16
  217.5 17.7 %collective-permute-done.15 = bf16[768,1024]{1,0:T(8,128)(2,1)S(1)} collective-permute-done((bf16[768,1024]{1,0:T(8,128)(2,1)S(1)}, bf16[768,1024]{1,0:T(8,128)(2,1)S(1)}, u32[]{:S(2)}, u32[]{:S(2)}) %collective-permute-start.15) | collective-permute-done | bytes 1572896 | tf_op jit(solution)/shard_map/ppermute | solution.py:12
  235.2 1.4 fusion.18
  236.7 7.7 %collective-permute-done.13 = bf16[768,1024]{1,0:T(8,128)(2,1)S(1)} collective-permute-done((bf16[768,1024]{1,0:T(8,128)(2,1)S(1)}, bf16[768,1024]{1,0:T(8,128)(2,1)S(1)}, u32[]{:S(2)}, u32[]{:S(2)}) %collective-permute-start.13) | collective-permute-done | bytes 1572896 | tf_op jit(solution)/shard_map/ppermute | solution.py:12
  244.4 5.0 %select_reduce_fusion.11 = (f32[768]{0:T(1024)S(1)}, f32[768]{0:T(1024)S(1)}, f32[768]{0:T(1024)S(1)}, f32[768]{0:T(1024)S(1)}, f32[768]{0:T(1024)S(1)}, /*index=5*/f32[768]{0:T(1024)S(1)}) fusion(f32[768,768]{0,1:T(8,128)S(1)} %fusion.17, s32[768]{0:T(1024)S(1)} %broadcast_in_dim_reshape.2, s32[768]{0:T(1024)S(1)} %collective-permute-done.10, ...), kind=kOutput, calls=%fused_computation.32 | convolution fusion | flops 1223880192 | bytes 7898112 | tf_op jit(solution)/shard_map/dot_general | solution.py:16
  249.4 0.1 reshape.302
  249.5 0.1 reshape.301
  249.7 0.7 copy.20
  250.4 10.9 %all-to-all-start.2 = ((f32[2,128,6]{2,0,1:T(2,128)}), f32[2,128,6]{2,0,1:T(2,128)S(1)}, u32[]{:S(2)}, u32[]{:S(2)}) async-start(f32[2,128,6]{2,0,1:T(2,128)} %copy.20), calls=%async_computation.2 | async-start | bytes 262144 | tf_op jit(solution)/shard_map/all_to_all | solution.py:81
  261.3 10.0 %all-to-all-done.2 = f32[2,128,6]{2,0,1:T(2,128)S(1)} async-done(((f32[2,128,6]{2,0,1:T(2,128)}), f32[2,128,6]{2,0,1:T(2,128)S(1)}, u32[]{:S(2)}, u32[]{:S(2)}) %all-to-all-start.2) | async-done | bytes 6176 | tf_op jit(solution)/shard_map/all_to_all | solution.py:81
  271.3 0.1 reshape.294
  271.4 0.2 copy.22
  271.6 1.1 gather_fusion
  272.8 0.8 slice_reduce_fusion
  (24 shorter events, 0.2 us)
Async XLA Ops:
  0.6 1.5 copy-start.1
  0.6 1.5 copy-start
  51.4 56.5 %collective-permute-start.3 = (bf16[768,1024]{1,0:T(8,128)(2,1)S(1)}, bf16[768,1024]{1,0:T(8,128)(2,1)}, u32[]{:S(2)}, u32[]{:S(2)}) collective-permute-start(bf16[768,1024]{1,0:T(8,128)(2,1)S(1)} %reshape.293), channel_id=1, source_target_pairs={{1,0},{2,1},{3,2},{4,3},{5,4},{6,5},{7,6},{8,7},{9,8},{10,9},{11,1... | collective-permute-start | bytes 4718600 | tf_op jit(solution)/shard_map/ppermute | solution.py:12
  55.0 61.7 %collective-permute-start.1 = (bf16[768,1024]{1,0:T(8,128)(2,1)S(1)}, bf16[768,1024]{1,0:T(8,128)(2,1)}, u32[]{:S(2)}, u32[]{:S(2)}) collective-permute-start(bf16[768,1024]{1,0:T(8,128)(2,1)S(1)} %reshape.293), channel_id=1, source_target_pairs={{31,0},{0,1},{1,2},{2,3},{3,4},{4,5},{5,6},{6,7},{7,8},{8,9},{9,10... | collective-permute-start | bytes 4718600 | tf_op jit(solution)/shard_map/ppermute | solution.py:12
  99.5 15.6 %collective-permute-start.2 = (s32[768]{0:T(1024)S(1)}, s32[768]{0:T(1024)S(1)}, u32[]{:S(2)}, u32[]{:S(2)}) collective-permute-start(s32[768]{0:T(1024)S(1)} %broadcast_in_dim_reshape.2), channel_id=1, source_target_pairs={{1,0},{2,1},{3,2},{4,3},{5,4},{6,5},{7,6},{8,7},{9,8},{10,9},{11,1... | collective-permute-start | bytes 9224 | tf_op jit(solution)/shard_map/ppermute | solution.py:12
  99.7 8.2 %collective-permute-start = (s32[768]{0:T(1024)S(1)}, s32[768]{0:T(1024)S(1)}, u32[]{:S(2)}, u32[]{:S(2)}) collective-permute-start(s32[768]{0:T(1024)S(1)} %broadcast_in_dim_reshape.2), channel_id=1, source_target_pairs={{31,0},{0,1},{1,2},{2,3},{3,4},{4,5},{5,6},{6,7},{7,8},{8,9},{9,10... | collective-permute-start | bytes 9224 | tf_op jit(solution)/shard_map/ppermute | solution.py:12
  107.9 8.2 %collective-permute-start.4 = (s32[768]{0:T(1024)S(1)}, s32[768]{0:T(1024)S(1)}, u32[]{:S(2)}, u32[]{:S(2)}) collective-permute-start(s32[768]{0:T(1024)S(1)} %collective-permute-done), channel_id=1, source_target_pairs={{31,0},{0,1},{1,2},{2,3},{3,4},{4,5},{5,6},{6,7},{7,8},{8,9},{9,10... | collective-permute-start | bytes 9224 | tf_op jit(solution)/shard_map/ppermute | solution.py:12
  107.9 55.9 %collective-permute-start.7 = (bf16[768,1024]{1,0:T(8,128)(2,1)}, bf16[768,1024]{1,0:T(8,128)(2,1)S(1)}, u32[]{:S(2)}, u32[]{:S(2)}) collective-permute-start(bf16[768,1024]{1,0:T(8,128)(2,1)} %collective-permute-done.3), channel_id=1, source_target_pairs={{1,0},{2,1},{3,2},{4,3},{5,4},{6,5},{7,6},{8,7},{9,8},{10,9},{11,1... | collective-permute-start | bytes 4718600 | tf_op jit(solution)/shard_map/ppermute | solution.py:12
  115.1 31.9 %collective-permute-start.6 = (s32[768]{0:T(1024)S(1)}, s32[768]{0:T(1024)S(1)}, u32[]{:S(2)}, u32[]{:S(2)}) collective-permute-start(s32[768]{0:T(1024)S(1)} %collective-permute-done.2), channel_id=1, source_target_pairs={{1,0},{2,1},{3,2},{4,3},{5,4},{6,5},{7,6},{8,7},{9,8},{10,9},{11,1... | collective-permute-start | bytes 9224 | tf_op jit(solution)/shard_map/ppermute | solution.py:12
  116.1 38.8 %collective-permute-start.8 = (s32[768]{0:T(1024)S(1)}, s32[768]{0:T(1024)S(1)}, u32[]{:S(2)}, u32[]{:S(2)}) collective-permute-start(s32[768]{0:T(1024)S(1)} %collective-permute-done.4), channel_id=1, source_target_pairs={{31,0},{0,1},{1,2},{2,3},{3,4},{4,5},{5,6},{6,7},{7,8},{8,9},{9,10... | collective-permute-start | bytes 9224 | tf_op jit(solution)/shard_map/ppermute | solution.py:12
  116.7 56.2 %collective-permute-start.5 = (bf16[768,1024]{1,0:T(8,128)(2,1)}, bf16[768,1024]{1,0:T(8,128)(2,1)S(1)}, u32[]{:S(2)}, u32[]{:S(2)}) collective-permute-start(bf16[768,1024]{1,0:T(8,128)(2,1)} %collective-permute-done.1), channel_id=1, source_target_pairs={{31,0},{0,1},{1,2},{2,3},{3,4},{4,5},{5,6},{6,7},{7,8},{8,9},{9,10... | collective-permute-start | bytes 4718600 | tf_op jit(solution)/shard_map/ppermute | solution.py:12
  147.0 8.7 %collective-permute-start.10 = (s32[768]{0:T(1024)S(1)}, s32[768]{0:T(1024)S(1)}, u32[]{:S(2)}, u32[]{:S(2)}) collective-permute-start(s32[768]{0:T(1024)S(1)} %collective-permute-done.6), channel_id=1, source_target_pairs={{1,0},{2,1},{3,2},{4,3},{5,4},{6,5},{7,6},{8,7},{9,8},{10,9},{11,1... | collective-permute-start | bytes 9224 | tf_op jit(solution)/shard_map/ppermute | solution.py:12
  154.9 8.2 %collective-permute-start.12 = (s32[768]{0:T(1024)S(1)}, s32[768]{0:T(1024)S(1)}, u32[]{:S(2)}, u32[]{:S(2)}) collective-permute-start(s32[768]{0:T(1024)S(1)} %collective-permute-done.8), channel_id=1, source_target_pairs={{31,0},{0,1},{1,2},{2,3},{3,4},{4,5},{5,6},{6,7},{7,8},{8,9},{9,10... | collective-permute-start | bytes 9224 | tf_op jit(solution)/shard_map/ppermute | solution.py:12
  155.6 8.2 %collective-permute-start.14 = (s32[768]{0:T(1024)S(1)}, s32[768]{0:T(1024)S(1)}, u32[]{:S(2)}, u32[]{:S(2)}) collective-permute-start(s32[768]{0:T(1024)S(1)} %collective-permute-done.10), channel_id=1, source_target_pairs={{1,0},{2,1},{3,2},{4,3},{5,4},{6,5},{7,6},{8,7},{9,8},{10,9},{11,1... | collective-permute-start | bytes 9224 | tf_op jit(solution)/shard_map/ppermute | solution.py:12
  163.8 36.0 %collective-permute-start.11 = (bf16[768,1024]{1,0:T(8,128)(2,1)S(1)}, bf16[768,1024]{1,0:T(8,128)(2,1)S(1)}, u32[]{:S(2)}, u32[]{:S(2)}) collective-permute-start(bf16[768,1024]{1,0:T(8,128)(2,1)S(1)} %collective-permute-done.7), channel_id=1, source_target_pairs={{1,0},{2,1},{3,2},{4,3},{5,4},{6,5},{7,6},{8,7},{9,8},{10,9},{11,1... | collective-permute-start | bytes 4718600 | tf_op jit(solution)/shard_map/ppermute | solution.py:12
  172.9 36.3 %collective-permute-start.9 = (bf16[768,1024]{1,0:T(8,128)(2,1)S(1)}, bf16[768,1024]{1,0:T(8,128)(2,1)S(1)}, u32[]{:S(2)}, u32[]{:S(2)}) collective-permute-start(bf16[768,1024]{1,0:T(8,128)(2,1)S(1)} %collective-permute-done.5), channel_id=1, source_target_pairs={{31,0},{0,1},{1,2},{2,3},{3,4},{4,5},{5,6},{6,7},{7,8},{8,9},{9,10... | collective-permute-start | bytes 4718600 | tf_op jit(solution)/shard_map/ppermute | solution.py:12
  199.9 35.4 %collective-permute-start.15 = (bf16[768,1024]{1,0:T(8,128)(2,1)S(1)}, bf16[768,1024]{1,0:T(8,128)(2,1)S(1)}, u32[]{:S(2)}, u32[]{:S(2)}) collective-permute-start(bf16[768,1024]{1,0:T(8,128)(2,1)S(1)} %collective-permute-done.11), channel_id=1, source_target_pairs={{1,0},{2,1},{3,2},{4,3},{5,4},{6,5},{7,6},{8,7},{9,8},{10,9},{11,1... | collective-permute-start | bytes 4718600 | tf_op jit(solution)/shard_map/ppermute | solution.py:12
  209.2 35.2 %collective-permute-start.13 = (bf16[768,1024]{1,0:T(8,128)(2,1)S(1)}, bf16[768,1024]{1,0:T(8,128)(2,1)S(1)}, u32[]{:S(2)}, u32[]{:S(2)}) collective-permute-start(bf16[768,1024]{1,0:T(8,128)(2,1)S(1)} %collective-permute-done.9), channel_id=1, source_target_pairs={{31,0},{0,1},{1,2},{2,3},{3,4},{4,5},{5,6},{6,7},{7,8},{8,9},{9,10... | collective-permute-start | bytes 4718600 | tf_op jit(solution)/shard_map/ppermute | solution.py:12
  250.4 20.8 %all-to-all-start.2 = ((f32[2,128,6]{2,0,1:T(2,128)}), f32[2,128,6]{2,0,1:T(2,128)S(1)}, u32[]{:S(2)}, u32[]{:S(2)}) async-start(f32[2,128,6]{2,0,1:T(2,128)} %copy.20), calls=%async_computation.2 | async-start | bytes 262144 | tf_op jit(solution)/shard_map/all_to_all | solution.py:81
where the time goes:
time: 274 us
  waiting for transfers between devices  93.1 us (34%)
  blocking collectives  80.3 us (29%)
  starting transfers between devices  55.1 us (20%)
  matrix products  25.9 us (9%)
  local copies, waits for them, and re-layouts  12.4 us (5%)
  other arithmetic  5.92 us (2%)
    ppermute x16, waiting for transfers between devices, passed_along(): return lax.ppermute(block, axis, route)  83.1 us
    ppermute x16, starting transfers between devices, passed_along(): return lax.ppermute(block, axis, route)  44.2 us
    all_to_all x1, blocking collectives, body(): lax.all_to_all(send_rows.reshape(total_devs, capacity, feat_width), ('gro...  40.5 us
    all_to_all x1, blocking collectives, body(): lax.all_to_all(send_ranks, ('group', 'blk'), split_axis=0, concat_axis=0,...  39.9 us
    dot_general x9, matrix products, compare(): lax.dot_general(left, right, (((1,), (1,)), ((), ())), preferred_element_...  25.9 us
    all_to_all x1, starting transfers between devices, body(): lax.all_to_all(results, ('group', 'blk'), split_axis=1, concat_axis=1, ti...  10.9 us
    all_to_all x1, waiting for transfers between devices, body(): lax.all_to_all(results, ('group', 'blk'), split_axis=1, concat_axis=1, ti...  9.97 us
  transfers between devices with their start and end apart: 17, of which 10 were waited for; matrix products, arithmetic and copies ran while one was open for 9% of the time, Pallas kernels for 0%

commit v1 on v0

v1 whole, which is shorter than its diff:
```python
import jax
import jax.numpy as jnp
from jax import lax
from jax.experimental import pallas as pl
from jax.experimental.pallas import tpu as pltpu
from jax.sharding import PartitionSpec as P

MESH = pl.DeviceIdType.MESH
F32 = jnp.float32
BF16 = jnp.bfloat16

D = 1024
ROWS = 384
SLOTS = 768
CH = 3
CR = 256
COL = 8
PLANE = 16


def iota(shape, dim):
    return lax.broadcasted_iota(jnp.int32, shape, dim)


def hot(mask):
    return jnp.where(mask, 1.0, 0.0).astype(BF16)


def pick(x, onehot, parts):
    rows = x.shape[0]
    pieces = []
    for _ in range(parts):
        piece = x.astype(BF16)
        pieces.append(piece)
        x = x - piece.astype(F32)
    out = jnp.dot(jnp.concatenate(pieces, axis=0), onehot, preferred_element_type=F32)
    total = out[(parts - 1) * rows :]
    for p in range(parts - 2, -1, -1):
        total = total + out[p * rows : (p + 1) * rows]
    return total


def place(x, z):
    return x * 4 + jnp.where(x % 2 == 0, z, 3 - z)


def chip(s):
    x = s // 4
    z = s % 4
    return x, jnp.where(x % 2 == 0, z, 3 - z)


def device(x, y, z, core):
    return ((y % 2) * 2 + core, (y // 2) * 16 + x * 4 + z)


def kernel(
    emb, meta, out_early, out_late,
    send1, recv1, send2, own, left, right,
    rk1s, rk1r, rk2s, rk2r, rk_own, rk_left, rk_right,
    lr_own, lr_left, acc_left, acc_right,
    part_s, part_r, b1s, b1r, b2s, b2r, m_home, m_back,
    ss1, rs1, ss2, rs2, ssr1, rsr1, ssr2, rsr2, ssring, rsring, ssrk, rsrk,
    sspart, rspart, ssb1, rsb1, ssb2, rsb2, loc1, loc2,
):
    grp = lax.axis_index("group")
    blk = lax.axis_index("blk")
    x, y, z, core = (blk // 4) % 4, (blk // 16) * 2 + grp // 2, blk % 4, grp % 2
    me = y * 2 + core
    s = place(x, z)

    def col_dev(g):
        return device(x, g // 2, z, g % 2)

    def ring_dev(t, k):
        tx, tz = chip(t)
        return device(tx, y, tz, k)

    up = (s + 1) % PLANE
    down = (s + PLANE - 1) % PLANE
    diag = ring_dev(jnp.where(core == 0, down, up), 1 - core)
    sibling = ring_dev(s, 1 - core)

    barrier = pltpu.get_barrier_semaphore()

    def greet_col(i, c):
        pl.semaphore_signal(barrier, inc=1, device_id=col_dev((me + i) % COL), device_id_type=MESH)
        return c

    def greet_plane(i, c):
        pl.semaphore_signal(barrier, inc=1, device_id=ring_dev((s + i) % PLANE, core), device_id_type=MESH)
        return c

    lax.fori_loop(1, COL, greet_col, 0)
    lax.fori_loop(1, PLANE, greet_plane, 0)
    pl.semaphore_signal(barrier, inc=1, device_id=diag, device_id_type=MESH)

    e = emb[...]
    mean_square = jnp.mean(e * e, axis=-1, keepdims=True)
    unit = (e * lax.rsqrt(mean_square + 1e-06) * D ** (-0.5)).astype(BF16)
    target = meta[0:1, :]
    rank = meta[1:2, :].astype(F32) + 1.0
    spread = iota((128, ROWS), 0) == target
    before = hot(iota((ROWS, ROWS), 0) < iota((ROWS, ROWS), 1))
    count = jnp.dot(hot(spread), before, preferred_element_type=F32)
    slot = jnp.sum(jnp.where(spread, count, 0.0), axis=0, keepdims=True).astype(jnp.int32)
    block = target % 32
    goal = (target // 32) * 2 + block % 2
    ring = block // 2
    chunk = slot // 2
    at_goal = iota((COL, ROWS), 0) == goal
    spot = chunk * 32 + ring * 2 + slot % 2
    at_spot = hot(iota((128, ROWS), 0) == spot)
    ranks16 = jnp.concatenate([jnp.where(at_goal, rank, 0.0), jnp.zeros((COL, ROWS), F32)], axis=0)
    hi = ranks16.astype(BF16)
    lo = (ranks16 - hi.astype(F32)).astype(BF16)
    dims = (((1,), (1,)), ((), ()))
    packed = lax.dot_general(hi, at_spot, dims, preferred_element_type=F32) + lax.dot_general(
        lo, at_spot, dims, preferred_element_type=F32
    )
    for g in range(COL):
        rk1s[g] = packed[g : g + 1]

    def fill(q):
        index = jnp.where(chunk == q, goal * 32 + ring * 2 + slot % 2, -1)
        select = hot(iota((CR, ROWS), 0) == index)
        for n in range(4):
            cols = slice(n * 256, (n + 1) * 256)
            rows = jnp.dot(select, unit[:, cols], preferred_element_type=F32).astype(BF16)
            send1[q, :, :, cols] = rows.reshape(COL, 32, 256)

    fill(0)
    pl.semaphore_wait(barrier, COL - 1 + PLANE - 1 + 1)

    def rk1(i):
        g = (me + i) % COL
        return pltpu.make_async_remote_copy(
            src_ref=rk1s.at[g], dst_ref=rk1r.at[me], send_sem=ssr1.at[i], recv_sem=rsr1.at[i],
            device_id=col_dev(g), device_id_type=MESH,
        )

    def row1(q, i):
        g = (me + i) % COL
        return pltpu.make_async_remote_copy(
            src_ref=send1.at[q, g], dst_ref=recv1.at[q, me], send_sem=ss1.at[q, i], recv_sem=rs1.at[q, i],
            device_id=col_dev(g), device_id_type=MESH,
        )

    def row2(q, i):
        t = (s + i) % PLANE
        return pltpu.make_async_remote_copy(
            src_ref=send2.at[q, t], dst_ref=own.at[q, s], send_sem=ss2.at[q, i], recv_sem=rs2.at[q, i],
            device_id=ring_dev(t, core), device_id_type=MESH,
        )

    def rk2(i):
        t = (s + i) % PLANE
        return pltpu.make_async_remote_copy(
            src_ref=rk2s.at[t], dst_ref=rk2r.at[s], send_sem=ssr2.at[i], recv_sem=rsr2.at[i],
            device_id=ring_dev(t, core), device_id_type=MESH,
        )

    def each(first, last, act):
        def step(i, c):
            act(i)
            return c

        lax.fori_loop(first, last, step, 0)

    each(1, COL, lambda i: rk1(i).start())
    for q in range(CH):
        if q:
            fill(q)
        each(1, COL, lambda i: row1(q, i).start())
        pltpu.make_async_copy(send1.at[q, me], recv1.at[q, me], loc1.at[q]).start()

    rk1r[me] = rk1s[me]
    each(1, COL, lambda i: rk1(i).wait_recv())
    seen = jnp.concatenate([rk1r[g] for g in range(COL)], axis=0)
    lane = iota((PLANE, COL, 128), 2)
    wide = jnp.where((lane % 32) // 2 == iota((PLANE, COL, 128), 0), seen[None], 0.0)
    a, b = iota((128, 128), 0), iota((128, 128), 1)
    fold = hot((a // 32 == b // 16) & (a % 2 == b % 2) & (a < 96) & (b < 48))
    wide = pick(wide.reshape(128, 128), fold, 2).reshape(PLANE, COL, 128)
    wide = jnp.sum(jnp.where((lane % 16) // 2 == iota((PLANE, COL, 128), 1), wide, 0.0), axis=1)
    for t in range(PLANE):
        rk2s[t] = wide[t : t + 1]
    each(1, PLANE, lambda i: rk2(i).start())
    rk2r[s] = rk2s[s]

    turn = hot(iota((CR, CR), 1) == (iota((CR, CR), 0) % 16 // 2) * 32 + (iota((CR, CR), 0) // 16) * 2 + iota((CR, CR), 0) % 2)

    def regroup(q):
        each(1, COL, lambda i: row1(q, i).wait_recv())
        pltpu.make_async_copy(send1.at[q, me], recv1.at[q, me], loc1.at[q]).wait()
        for n in range(4):
            cols = slice(n * 256, (n + 1) * 256)
            rows = recv1[q, :, :, cols].reshape(CR, 256)
            rows = jnp.dot(turn, rows, preferred_element_type=F32).astype(BF16)
            send2[q, :, :, cols] = rows.reshape(PLANE, 16, 256)
        each(1, PLANE, lambda i: row2(q, i).start())
        pltpu.make_async_copy(send2.at[q, s], own.at[q, s], loc2.at[q]).start()

    def to_up(q):
        return pltpu.make_async_remote_copy(
            src_ref=own.at[q], dst_ref=left.at[core, q], send_sem=ssring.at[0, q], recv_sem=rsring.at[0, q],
            device_id=ring_dev(up, core), device_id_type=MESH,
        )

    def to_down(q):
        return pltpu.make_async_remote_copy(
            src_ref=own.at[q], dst_ref=right.at[q], send_sem=ssring.at[1, q], recv_sem=rsring.at[1, q],
            device_id=ring_dev(down, core), device_id_type=MESH,
        )

    def to_sibling(q, k):
        return pltpu.make_async_remote_copy(
            src_ref=own.at[q] if k == 0 else left.at[1, q], dst_ref=left.at[k, q],
            send_sem=ssring.at[2, q], recv_sem=rsring.at[2, q],
            device_id=sibling, device_id_type=MESH,
        )

    def rk_up():
        return pltpu.make_async_remote_copy(
            src_ref=rk_own, dst_ref=rk_left.at[core], send_sem=ssrk.at[0], recv_sem=rsrk.at[0],
            device_id=ring_dev(up, core), device_id_type=MESH,
        )

    def rk_down():
        return pltpu.make_async_remote_copy(
            src_ref=rk_own, dst_ref=rk_right, send_sem=ssrk.at[1], recv_sem=rsrk.at[1],
            device_id=ring_dev(down, core), device_id_type=MESH,
        )

    def rk_sibling(k):
        return pltpu.make_async_remote_copy(
            src_ref=rk_own if k == 0 else rk_left.at[1], dst_ref=rk_left.at[k], send_sem=ssrk.at[2], recv_sem=rsrk.at[2],
            device_id=sibling, device_id_type=MESH,
        )

    def spread_out(q):
        each(1, PLANE, lambda i: row2(q, i).wait_recv())
        pltpu.make_async_copy(send2.at[q, s], own.at[q, s], loc2.at[q]).wait()
        to_up(q).start()
        to_down(q).start()

        @pl.when(core == 0)
        def _():
            to_sibling(q, 0).start()

    regroup(0)

    n_lane = iota((128, SLOTS), 1)
    m_home[...] = hot(iota((128, SLOTS), 0) == (n_lane // CR) * 16 + n_lane % 16)
    each(1, PLANE, lambda i: rk2(i).wait_recv())
    got = jnp.concatenate([rk2r[t] for t in range(PLANE)], axis=0)
    got = pick(got, m_home[...], 2)
    of_chip = (iota((PLANE, SLOTS), 1) % CR) // 16 == iota((PLANE, SLOTS), 0)
    got = jnp.sum(jnp.where(of_chip, got, 0.0), axis=0, keepdims=True)
    rk_own[...] = jnp.where(got > 0.0, got, jnp.nan)
    rk_up().start()
    rk_down().start()

    @pl.when(core == 0)
    def _():
        rk_sibling(0).start()

    regroup(1)
    spread_out(0)
    regroup(2)
    spread_out(1)
    spread_out(2)

    def stand(row):
        return jnp.broadcast_to(row, (128, SLOTS)).T.reshape(CH, CR, 128)

    lr_own[...] = stand(rk_own[...])
    acc_left[...] = jnp.full(acc_left.shape, -1.0, F32)
    acc_right[...] = jnp.full(acc_right.shape, -1.0, F32)

    def tile(rows, lr, other, rr, accs_left, accs_right):
        scores = lax.dot_general(rows, other, dims, preferred_element_type=F32)
        for h in range(2):
            half = scores[:, h * 128 : (h + 1) * 128]
            rank_right = rr[:, h * 128 : (h + 1) * 128]
            low = jnp.where(rank_right < lr, half, -1.0)
            high = jnp.where(rank_right > lr, half, -1.0)
            if accs_left is not None:
                accs_left[0][...] = jnp.maximum(accs_left[0][...], low)
                accs_left[1][...] = jnp.maximum(accs_left[1][...], high)
            cols = slice(h * 128, (h + 1) * 128)
            accs_right[0][:, cols] = jnp.maximum(accs_right[0][:, cols], jnp.max(high.reshape(32, 8, 128), axis=0))
            accs_right[1][:, cols] = jnp.maximum(accs_right[1][:, cols], jnp.max(low.reshape(32, 8, 128), axis=0))

    def lanes(ref, q):
        return ref[:, pl.ds(pl.multiple_of(q * CR, CR), CR)]

    def self_tile(i, c):
        qa, qb = i // CH, i % CH
        tile(
            own[qa].reshape(CR, D), lr_own[qa], own[qb].reshape(CR, D), lanes(rk_own, qb),
            None, (acc_right.at[0, 0, qb], acc_right.at[0, 1, qb]),
        )
        return c

    lax.fori_loop(0, CH * CH, self_tile, 0)

    rk_up().wait_recv()

    @pl.when(core == 1)
    def _():
        rk_sibling(1).start()

    rk_down().wait_recv()
    rk_sibling(0).wait_recv()
    for a in range(2):
        lr_left[a] = stand(rk_left[a])
    n_row, l_col = iota((2 * SLOTS, 128), 0), iota((2 * SLOTS, 128), 1)
    m_back[...] = hot(
        (l_col < 96) & (l_col // 48 == n_row // SLOTS) & ((l_col % 48) // 16 == (n_row % SLOTS) // CR) & (l_col % 16 == n_row % 16)
    )

    def own_tile(a, qa, qb):
        tile(
            left[a, qa].reshape(CR, D), lr_left[a, qa], own[qb].reshape(CR, D), lanes(rk_own, qb),
            (acc_left.at[a, 0, qa], acc_left.at[a, 1, qa]), (acc_right.at[0, 0, qb], acc_right.at[0, 1, qb]),
        )

    def far_tile(a, qa, qb):
        tile(
            left[a, qa].reshape(CR, D), lr_left[a, qa], right[qb].reshape(CR, D), lanes(rk_right, qb),
            (acc_left.at[a, 0, qa], acc_left.at[a, 1, qa]), (acc_right.at[1, 0, qb], acc_right.at[1, 1, qb]),
        )

    for q in range(CH):
        to_up(q).wait_recv()

        @pl.when(core == 1)
        def _():
            to_sibling(q, 1).start()

        to_sibling(q, 0).wait_recv()
        each(0, 2 * CH, lambda i: own_tile(i // CH, q, i % CH))
        to_down(q).wait_recv()
        each(0, 2 * (q + 1), lambda i: far_tile(i // (q + 1), q, i % (q + 1)))
        if q:
            each(0, 2 * q, lambda i: far_tile(i // q, i % q, q))

    def lie(acc):
        return jnp.max(acc.reshape(SLOTS, 128).T, axis=0, keepdims=True)

    def flat(acc):
        return jnp.concatenate([jnp.max(acc[q], axis=0, keepdims=True) for q in range(CH)], axis=1)

    def part(m, to):
        return pltpu.make_async_remote_copy(
            src_ref=part_s.at[m], dst_ref=part_r.at[m], send_sem=sspart.at[m], recv_sem=rspart.at[m],
            device_id=to, device_id_type=MESH,
        )

    to0 = ring_dev(down, core)
    to1 = ring_dev(jnp.where(core == 0, down, s), 1 - core)
    to2 = ring_dev(up, core)
    for el in range(2):
        part_s[2, el : el + 1, :] = flat(acc_right[1, el])
    part(2, to2).start()
    for m in range(2):
        for el in range(2):
            part_s[m, el : el + 1, :] = lie(acc_left[core if m == 0 else 1 - core, el])
        part(m, to0 if m == 0 else to1).start()
    mine = [flat(acc_right[0, el]) for el in range(2)]
    part(2, to2).wait_recv()
    part(0, to0).wait_recv()
    part(1, to1).wait_recv()
    for m in range(3):
        for el in range(2):
            mine[el] = jnp.maximum(mine[el], part_r[m, el : el + 1, :])

    def back1(i):
        t = (s + i) % PLANE
        return pltpu.make_async_remote_copy(
            src_ref=b1s.at[t], dst_ref=b1r.at[s], send_sem=ssb1.at[i], recv_sem=rsb1.at[i],
            device_id=ring_dev(t, core), device_id_type=MESH,
        )

    def back2(i):
        g = (me + i) % COL
        return pltpu.make_async_remote_copy(
            src_ref=b2s.at[g], dst_ref=b2r.at[me], send_sem=ssb2.at[i], recv_sem=rsb2.at[i],
            device_id=col_dev(g), device_id_type=MESH,
        )

    both = jnp.concatenate([jnp.where(of_chip, m, 0.0) for m in mine], axis=1)
    both = pick(both, m_back[...], 3)
    for t in range(PLANE):
        b1s[t] = both[t : t + 1]
    each(1, PLANE, lambda i: back1(i).start())
    b1r[s] = b1s[s]
    a, b = iota((128, 256), 0), iota((128, 256), 1)
    unfold = hot(
        (a // 48 == b // 128) & ((a % 48) // 16 == (b % 128) // 32) & (a % 2 == b % 2) & (b % 128 < 96)
    )
    each(1, PLANE, lambda i: back1(i).wait_recv())
    got = jnp.concatenate([b1r[t] for t in range(PLANE)], axis=0)
    wide = jnp.where((iota((COL, PLANE, 128), 2) % 16) // 2 == iota((COL, PLANE, 128), 0), got[None], 0.0)
    wide = pick(wide.reshape(128, 128), unfold, 3).reshape(COL, PLANE, 256)
    wide = jnp.where((iota((COL, PLANE, 256), 2) % 32) // 2 == iota((COL, PLANE, 256), 1), wide, 0.0)
    wide = jnp.sum(wide, axis=1)
    for g in range(COL):
        b2s[g] = wide[g : g + 1]
    each(1, COL, lambda i: back2(i).start())
    b2r[me] = b2s[me]
    each(1, COL, lambda i: back2(i).wait_recv())
    got = jnp.concatenate([b2r[g] for g in range(COL)], axis=0)
    got = jnp.concatenate([got[:, :128], got[:, 128:]], axis=0)
    got = pick(got, at_spot, 3)
    out_early[...] = jnp.sum(jnp.where(at_goal, got[:COL], 0.0), axis=0, keepdims=True)
    out_late[...] = jnp.sum(jnp.where(at_goal, got[COL:], 0.0), axis=0, keepdims=True)

    each(1, COL, lambda i: rk1(i).wait_send())
    each(1, PLANE, lambda i: rk2(i).wait_send())
    for q in range(CH):
        each(1, COL, lambda i: row1(q, i).wait_send())
        each(1, PLANE, lambda i: row2(q, i).wait_send())
        to_up(q).wait_send()
        to_down(q).wait_send()
        to_sibling(q, 0).wait_send()
    rk_up().wait_send()
    rk_down().wait_send()
    rk_sibling(0).wait_send()
    part(0, to0).wait_send()
    part(1, to1).wait_send()
    part(2, to2).wait_send()
    each(1, PLANE, lambda i: back1(i).wait_send())
    each(1, COL, lambda i: back2(i).wait_send())


def body(embeddings, ranks, routes):
    meta = jnp.stack([routes[:, 0], ranks])
    dma = pltpu.SemaphoreType.DMA
    vm = pltpu.VMEM
    early, late = pl.pallas_call(
        kernel,
        out_shape=[jax.ShapeDtypeStruct((1, ROWS), F32)] * 2,
        in_specs=[pl.BlockSpec(memory_space=vm)] * 2,
        out_specs=[pl.BlockSpec(memory_space=vm)] * 2,
        scratch_shapes=[
            vm((CH, COL, 32, D), BF16),
            vm((CH, COL, 32, D), BF16),
            vm((CH, PLANE, 16, D), BF16),
            vm((CH, PLANE, 16, D), BF16),
            vm((2, CH, PLANE, 16, D), BF16),
            vm((CH, PLANE, 16, D), BF16),
            vm((COL, 1, 128), F32),
            vm((COL, 1, 128), F32),
            vm((PLANE, 1, 128), F32),
            vm((PLANE, 1, 128), F32),
            vm((1, SLOTS), F32),
            vm((2, 1, SLOTS), F32),
            vm((1, SLOTS), F32),
            vm((CH, CR, 128), F32),
            vm((2, CH, CR, 128), F32),
            vm((2, 2, CH, CR, 128), F32),
            vm((2, 2, CH, 8, CR), F32),
            vm((3, 2, SLOTS), F32),
            vm((3, 2, SLOTS), F32),
            vm((PLANE, 1, 128), F32),
            vm((PLANE, 1, 128), F32),
            vm((COL, 1, 256), F32),
            vm((COL, 1, 256), F32),
            vm((128, SLOTS), BF16),
            vm((2 * SLOTS, 128), BF16),
            dma((CH, COL)), dma((CH, COL)),
            dma((CH, PLANE)), dma((CH, PLANE)),
            dma((COL,)), dma((COL,)),
            dma((PLANE,)), dma((PLANE,)),
            dma((3, CH)), dma((3, CH)),
            dma((3,)), dma((3,)),
            dma((3,)), dma((3,)),
            dma((PLANE,)), dma((PLANE,)),
            dma((COL,)), dma((COL,)),
            dma((CH,)), dma((CH,)),
        ],
        compiler_params=pltpu.CompilerParams(
            collective_id=0, has_side_effects=True, vmem_limit_bytes=48 * 2**20
        ),
    )(embeddings, meta)
    return early.reshape(ROWS), late.reshape(ROWS)


def solution(mesh):
    placed = (P(("group", "blk"), None), P(("group", "blk")), P(("group", "blk"), None))
    return jax.shard_map(
        body,
        mesh=mesh,
        in_specs=placed,
        out_specs=(P(("group", "blk")), P(("group", "blk"))),
        check_vma=False,
    )
```

time: 274 us -> 97.2 us (0.35)
  waiting for transfers between devices: 93.1 us -> 0 us
  Pallas kernels: 0 us -> 92.4 us
  blocking collectives: 80.3 us -> 0 us
  starting transfers between devices: 55.1 us -> 0 us
  matrix products: 25.9 us -> 0 us
  local copies, waits for them, and re-layouts: 12.4 us -> 2.09 us
  other arithmetic: 5.92 us -> 1.88 us
    pallas_call x0 -> x1, Pallas kernels: none -> 92.4 us  [body(): pl.pallas_call(kernel, out_shape=[jax.ShapeDtypeStruct((1, ROWS), F32)] *...]
    ppermute x16 -> x0, waiting for transfers between devices: 83.1 us -> none  [passed_along(): return lax.ppermute(block, axis, route)]
    all_to_all x2 -> x0, blocking collectives: 80.3 us -> none  [the longest x1 40.5 us: body(): lax.all_to_all(send_rows.reshape(total_devs, capacity, feat_width), ('gro...]
    ppermute x16 -> x0, starting transfers between devices: 44.2 us -> none  [passed_along(): return lax.ppermute(block, axis, route)]
    dot_general x9 -> x0, matrix products: 25.9 us -> none  [compare(): lax.dot_general(left, right, (((1,), (1,)), ((), ())), preferred_element_...]
    all_to_all x1 -> x0, starting transfers between devices: 10.9 us -> none  [body(): lax.all_to_all(results, ('group', 'blk'), split_axis=1, concat_axis=1, ti...]
    all_to_all x1 -> x0, waiting for transfers between devices: 9.97 us -> none  [body(): lax.all_to_all(results, ('group', 'blk'), split_axis=1, concat_axis=1, ti...]
    reshape x4 -> x0, local copies, waits for them, and re-layouts: 5.41 us -> none  [the longest x1 2.6 us: body(): members = lax.all_to_all(send_rows.reshape(total_devs, capacity, feat_wid...]
  transfers between devices with their start and end apart: 17 -> 0, of which waited for: 10 -> 0; matrix products, arithmetic and copies ran while one was open for 9% -> 0% of each run, Pallas kernels for 0% -> 0%
where the time goes in v1:
time: 97.2 us; the launch traced here: 97 us
  Pallas kernels  92.4 us (95%)
  local copies, waits for them, and re-layouts  2.09 us (2%)
  other arithmetic  1.88 us (2%)
    pallas_call x1, Pallas kernels, body(): pl.pallas_call(kernel, out_shape=[jax.ShapeDtypeStruct((1, ROWS), F32)] *...  92.4 us

profile of v1, /device:TPU:1, one launch (start us, length us, event | category | flops | bytes accessed | tf_op | source)
XLA Modules:
  0.0 97.0 jit_solution(10688099166380452410)
XLA Ops:
  0.6 0.7 stack.6
  1.3 0.7 pad_add_fusion.meta
  2.0 0.0 copy-start
  2.0 1.4 %copy-done = f32[384,1024]{1,0:T(8,128)S(1)} copy-done((f32[384,1024]{1,0:T(8,128)S(1)}, f32[384,1024]{1,0:T(8,128)}, u32[]{:S(2)}) %copy-start) | copy-done | bytes 1572888
  3.4 92.4 %shard_map.50 = (f32[1,384]{1,0:T(1,128)S(1)}, f32[1,384]{1,0:T(1,128)S(1)}) custom-call(f32[384,1024]{1,0:T(8,128)S(1)} %copy-done, s32[2,384]{1,0:T(2,128)S(1)} %pad_add_fusion.meta), custom_call_target="tpu_custom_call" | custom-call | tf_op jit(solution)/shard_map/pallas_call | solution.py:442
  95.9 0.6 reduce
  96.5 0.6 reduce.1
Async XLA Ops:
  2.0 1.4 %copy-start = (f32[384,1024]{1,0:T(8,128)S(1)}, f32[384,1024]{1,0:T(8,128)}, u32[]{:S(2)}) copy-start(f32[384,1024]{1,0:T(8,128)} %emb.1) | copy-start | bytes 4718596

commit v2 on v1

v2 whole, which is shorter than its diff:
```python
import jax
import jax.numpy as jnp
from jax import lax
from jax.experimental import pallas as pl
from jax.experimental.pallas import tpu as pltpu
from jax.sharding import PartitionSpec as P

MESH = pl.DeviceIdType.MESH
F32 = jnp.float32
BF16 = jnp.bfloat16

D = 1024
HALF = 512
ROWS = 384
SLOTS = 768
CH = 3
CR = 256
COL = 8
PLANE = 16

RINGS = (
    (0, 4, 8, 12, 13, 1, 5, 9, 10, 14, 2, 6, 7, 11, 15, 3),
    (0, 1, 2, 3, 7, 4, 5, 6, 10, 11, 8, 9, 13, 14, 15, 12),
)
PLACES = tuple(tuple(r.index(n) for n in range(PLANE)) for r in RINGS)
UPS = tuple(tuple(r[(r.index(n) + 1) % PLANE] for n in range(PLANE)) for r in RINGS)
DOWNS = tuple(tuple(r[(r.index(n) - 1) % PLANE] for n in range(PLANE)) for r in RINGS)
STRAIGHT = 11
DETOURS = ((0, 1, 11, 14), (0, -1, 14, 16), (1, -1, 11, 14), (1, 1, 14, 16))


def iota(shape, dim):
    return lax.broadcasted_iota(jnp.int32, shape, dim)


def hot(mask):
    return jnp.where(mask, 1.0, 0.0).astype(BF16)


def pick(x, onehot, parts):
    rows = x.shape[0]
    pieces = []
    for _ in range(parts):
        piece = x.astype(BF16)
        pieces.append(piece)
        x = x - piece.astype(F32)
    out = jnp.dot(jnp.concatenate(pieces, axis=0), onehot, preferred_element_type=F32)
    total = out[(parts - 1) * rows :]
    for p in range(parts - 2, -1, -1):
        total = total + out[p * rows : (p + 1) * rows]
    return total


def look(tables, odd, index):
    found = index * 0
    for i in range(PLANE):
        found = jnp.where(index == i, jnp.where(odd == 1, tables[1][i], tables[0][i]), found)
    return found


def device(n, z, core):
    x, y = n // 4, n % 4
    return ((y % 2) * 2 + core, (y // 2) * 16 + x * 4 + z)


def each(first, last, act):
    def step(i, c):
        act(i)
        return c

    lax.fori_loop(first, last, step, 0)


def kernel(
    emb_hbm, ranks, routes, out_early, out_late,
    emb, send1a, recv1a, send2a, send1b, recv1b, send2b, recv2b, own, left, right, relay,
    rk1s, rk1r, rk2s, rk2r, rk_own, rk_left, rk_right,
    lr_own, lr_left, acc_left, acc_right,
    b1s, b1r, b2s, b2r, m_home, m_back,
    ss1a, rs1a, ss2a, rs2a, ss1b, rs1b, ss2b, rs2b, ssr1, rsr1, ssr2, rsr2,
    ssring, rsring, ssleg1, rsleg1, ssleg2, rsleg2, ssrk, rsrk,
    ssb1, rsb1, ssb2, rsb2, loc, emb_sem,
):
    load = pltpu.make_async_copy(emb_hbm, emb, emb_sem)
    load.start()
    grp = lax.axis_index("group")
    blk = lax.axis_index("blk")
    z, core = blk % 4, grp % 2
    n = ((blk // 4) % 4) * 4 + (blk // 16) * 2 + grp // 2
    me = core * 4 + z
    odd = z % 2
    s = look(PLACES, odd, n)
    up, down = look(UPS, odd, n), look(DOWNS, odd, n)
    beside = (look(UPS, 1 - odd, n), look(DOWNS, 1 - odd, n))

    def col_dev(g):
        return device(n, g % 4, g // 4)

    def plane_dev(t):
        return device(t, z, core)

    sibling = device(n, z, 1 - core)

    barrier = pltpu.get_barrier_semaphore()

    def greet(to):
        pl.semaphore_signal(barrier, inc=1, device_id=to, device_id_type=MESH)

    each(1, COL, lambda i: greet(col_dev((me + i) % COL)))
    each(1, PLANE, lambda i: greet(plane_dev((n + i) % PLANE)))
    for way, side, _, _ in DETOURS:
        greet(device(down if way == 0 else up, (z + side) % 4, core))

    target = routes[...].reshape(1, ROWS)
    rank = ranks[...].reshape(1, ROWS).astype(F32) + 1.0
    spread = iota((128, ROWS), 0) == target
    before = hot(iota((ROWS, ROWS), 0) < iota((ROWS, ROWS), 1))
    count = jnp.dot(hot(spread), before, preferred_element_type=F32)
    slot = jnp.sum(jnp.where(spread, count, 0.0), axis=0, keepdims=True).astype(jnp.int32)
    cluster, block = target // 32, target % 32
    goal = (block % 2) * 4 + cluster
    ring = block // 2
    to_chip = look(RINGS, cluster % 2, ring)
    chunk, two = slot // 2, slot % 2
    at_goal = iota((COL, ROWS), 0) == goal
    at_spot = hot(iota((128, ROWS), 0) == chunk * 32 + to_chip * 2 + two)
    at_back = hot(iota((128, ROWS), 0) == chunk * 32 + ring * 2 + two)
    ranks16 = jnp.concatenate([jnp.where(at_goal, rank, 0.0), jnp.zeros((COL, ROWS), F32)], axis=0)
    hi = ranks16.astype(BF16)
    lo = (ranks16 - hi.astype(F32)).astype(BF16)
    dims = (((1,), (1,)), ((), ()))
    packed = lax.dot_general(hi, at_spot, dims, preferred_element_type=F32) + lax.dot_general(
        lo, at_spot, dims, preferred_element_type=F32
    )
    for g in range(COL):
        rk1s[g] = packed[g : g + 1]
    load.wait()
    e = emb[...]
    mean_square = jnp.mean(e * e, axis=-1, keepdims=True)
    unit = (e * lax.rsqrt(mean_square + 1e-06) * D ** (-0.5)).astype(BF16)

    def fill(q):
        for index, ref, first, shape in (
            (goal * 32 + to_chip * 2 + two, send1a, 0, (COL, 32, 256)),
            (to_chip * 16 + goal * 2 + two, send1b, HALF, (PLANE, 16, 256)),
        ):
            select = hot(iota((CR, ROWS), 0) == jnp.where(chunk == q, index, -1))
            for c in range(0, HALF, 256):
                rows = jnp.dot(select, unit[:, first + c : first + c + 256], preferred_element_type=F32)
                ref[q, :, :, c : c + 256] = rows.astype(BF16).reshape(shape)

    def copy(src, dst, send, recv, to):
        return pltpu.make_async_remote_copy(
            src_ref=src, dst_ref=dst, send_sem=send, recv_sem=recv, device_id=to, device_id_type=MESH
        )

    def rk1(i):
        g = (me + i) % COL
        return copy(rk1s.at[g], rk1r.at[me], ssr1.at[i], rsr1.at[i], col_dev(g))

    def rk2(i):
        t = (n + i) % PLANE
        return copy(rk2s.at[t], rk2r.at[n], ssr2.at[i], rsr2.at[i], plane_dev(t))

    def row1a(q, i):
        g = (me + i) % COL
        return copy(send1a.at[q, g], recv1a.at[q, me], ss1a.at[q, i], rs1a.at[q, i], col_dev(g))

    def row2a(q, i):
        t = (n + i) % PLANE
        return copy(send2a.at[q, t], own.at[q, n, :, pl.ds(0, HALF)], ss2a.at[q, i], rs2a.at[q, i], plane_dev(t))

    def row1b(q, i):
        t = (n + i) % PLANE
        return copy(send1b.at[q, t], recv1b.at[q, n], ss1b.at[q, i], rs1b.at[q, i], plane_dev(t))

    def row2b(q, i):
        g = (me + i) % COL
        return copy(send2b.at[q, g], recv2b.at[q, me], ss2b.at[q, i], rs2b.at[q, i], col_dev(g))

    def stay1a(q):
        return pltpu.make_async_copy(send1a.at[q, me], recv1a.at[q, me], loc.at[0, q])

    def stay2a(q):
        return pltpu.make_async_copy(send2a.at[q, n], own.at[q, n, :, pl.ds(0, HALF)], loc.at[1, q])

    def stay1b(q):
        return pltpu.make_async_copy(send1b.at[q, n], recv1b.at[q, n], loc.at[2, q])

    def stay2b(q):
        return pltpu.make_async_copy(send2b.at[q, me], recv2b.at[q, me], loc.at[3, q])

    fill(0)
    pl.semaphore_wait(barrier, COL - 1 + PLANE - 1 + len(DETOURS))
    each(1, COL, lambda i: rk1(i).start())
    for q in range(CH):
        if q:
            fill(q)
        each(1, COL, lambda i: row1a(q, i).start())
        each(1, PLANE, lambda i: row1b(q, i).start())
        stay1a(q).start()
        stay1b(q).start()

    rk1r[me] = rk1s[me]
    each(1, COL, lambda i: rk1(i).wait_recv())
    seen = jnp.concatenate([rk1r[g] for g in range(COL)], axis=0)
    lane = iota((PLANE, COL, 128), 2)
    wide = jnp.where((lane % 32) // 2 == iota((PLANE, COL, 128), 0), seen[None], 0.0)
    a, b = iota((128, 128), 0), iota((128, 128), 1)
    fold = hot((a // 32 == b // 16) & (a % 2 == b % 2) & (a < 96) & (b < 48))
    wide = pick(wide.reshape(128, 128), fold, 2).reshape(PLANE, COL, 128)
    wide = jnp.sum(jnp.where((lane % 16) // 2 == iota((PLANE, COL, 128), 1), wide, 0.0), axis=1)
    for t in range(PLANE):
        rk2s[t] = wide[t : t + 1]
    each(1, PLANE, lambda i: rk2(i).start())
    rk2r[n] = rk2s[n]

    a, b = iota((CR, CR), 0), iota((CR, CR), 1)
    by_chip = hot(b == (a % 16 // 2) * 32 + (a // 16) * 2 + a % 2)
    by_goal = hot(b == (a % 32 // 2) * 16 + (a // 32) * 2 + a % 2)

    def turn(order, src, dst, q, first, shape):
        for c in range(0, HALF, 256):
            rows = jnp.dot(order, src[q, :, :, c : c + 256].reshape(CR, 256), preferred_element_type=F32)
            dst[q, :, :, first + c : first + c + 256] = rows.astype(BF16).reshape(shape)

    def regroup(q):
        each(1, COL, lambda i: row1a(q, i).wait_recv())
        stay1a(q).wait()
        turn(by_chip, recv1a, send2a, q, 0, (PLANE, 16, 256))
        each(1, PLANE, lambda i: row2a(q, i).start())
        stay2a(q).start()
        each(1, PLANE, lambda i: row1b(q, i).wait_recv())
        stay1b(q).wait()
        turn(by_goal, recv1b, send2b, q, 0, (COL, 32, 256))
        each(1, COL, lambda i: row2b(q, i).start())
        stay2b(q).start()

    def straight(way, q):
        rows = pl.ds(0, STRAIGHT)
        return copy(
            own.at[q, rows], left.at[core, q, rows] if way == 0 else right.at[q, rows],
            ssring.at[way, q], rsring.at[way, q], plane_dev(up if way == 0 else down),
        )

    def leg1(d, q):
        _, side, first, last = DETOURS[d]
        return copy(
            own.at[q, pl.ds(first, last - first)], relay.at[d, q, pl.ds(0, last - first)],
            ssleg1.at[d, q], rsleg1.at[d, q], device(n, (z + side) % 4, core),
        )

    def leg2(d, q):
        way, side, first, last = DETOURS[d]
        rows = pl.ds(first, last - first)
        return copy(
            relay.at[d, q, pl.ds(0, last - first)], left.at[core, q, rows] if way == 0 else right.at[q, rows],
            ssleg2.at[d, q], rsleg2.at[d, q], device(beside[way], (z - side) % 4, core),
        )

    def to_sibling(q, k):
        return copy(own.at[q] if k == 0 else left.at[1, q], left.at[k, q], ssring.at[2, q], rsring.at[2, q], sibling)

    def rk_ring(way):
        return copy(
            rk_own, rk_left.at[core] if way == 0 else rk_right,
            ssrk.at[way], rsrk.at[way], plane_dev(up if way == 0 else down),
        )

    def rk_sibling(k):
        return copy(rk_own if k == 0 else rk_left.at[1], rk_left.at[k], ssrk.at[2], rsrk.at[2], sibling)

    def spread_out(q):
        each(1, COL, lambda i: row2b(q, i).wait_recv())
        stay2b(q).wait()
        turn(by_chip, recv2b, own, q, HALF, (PLANE, 16, 256))
        each(1, PLANE, lambda i: row2a(q, i).wait_recv())
        stay2a(q).wait()
        for d in range(len(DETOURS)):
            leg1(d, q).start()
        straight(0, q).start()
        straight(1, q).start()

        @pl.when(core == 0)
        def _():
            to_sibling(q, 0).start()

    def pass_on(q):
        for d in range(len(DETOURS)):
            leg1(d, q).wait_recv()
            leg2(d, q).start()

    regroup(0)

    n_lane = iota((128, SLOTS), 1)
    m_home[...] = hot(iota((128, SLOTS), 0) == (n_lane // CR) * 16 + n_lane % 16)
    each(1, PLANE, lambda i: rk2(i).wait_recv())
    got = jnp.concatenate([rk2r[t] for t in range(PLANE)], axis=0)
    got = pick(got, m_home[...], 2)
    of_chip = (iota((PLANE, SLOTS), 1) % CR) // 16 == iota((PLANE, SLOTS), 0)
    got = jnp.sum(jnp.where(of_chip, got, 0.0), axis=0, keepdims=True)
    rk_own[...] = jnp.where(got > 0.0, got, jnp.nan)
    rk_ring(0).start()
    rk_ring(1).start()

    @pl.when(core == 0)
    def _():
        rk_sibling(0).start()

    regroup(1)
    spread_out(0)
    regroup(2)
    spread_out(1)
    pass_on(0)
    spread_out(2)
    pass_on(1)

    def stand(row):
        return jnp.broadcast_to(row, (128, SLOTS)).T.reshape(CH, CR, 128)

    lr_own[...] = stand(rk_own[...])
    acc_left[...] = jnp.full(acc_left.shape, -1.0, F32)
    acc_right[...] = jnp.full(acc_right.shape, -1.0, F32)

    def tile(rows, lr, other, rr, accs_left, accs_right):
        scores = lax.dot_general(rows, other, dims, preferred_element_type=F32)
        for h in range(2):
            half = scores[:, h * 128 : (h + 1) * 128]
            rank_right = rr[:, h * 128 : (h + 1) * 128]
            low = jnp.where(rank_right < lr, half, -1.0)
            high = jnp.where(rank_right > lr, half, -1.0)
            if accs_left is not None:
                accs_left[0][...] = jnp.maximum(accs_left[0][...], low)
                accs_left[1][...] = jnp.maximum(accs_left[1][...], high)
            cols = slice(h * 128, (h + 1) * 128)
            accs_right[0][:, cols] = jnp.maximum(accs_right[0][:, cols], jnp.max(high.reshape(32, 8, 128), axis=0))
            accs_right[1][:, cols] = jnp.maximum(accs_right[1][:, cols], jnp.max(low.reshape(32, 8, 128), axis=0))

    def lanes(ref, q):
        return ref[:, pl.ds(pl.multiple_of(q * CR, CR), CR)]

    def self_tile(i):
        qa, qb = i // CH, i % CH
        tile(
            own[qa].reshape(CR, D), lr_own[qa], own[qb].reshape(CR, D), lanes(rk_own, qb),
            None, (acc_right.at[0, 0, qb], acc_right.at[0, 1, qb]),
        )

    each(0, CH * CH, self_tile)
    pass_on(2)

    rk_ring(0).wait_recv()

    @pl.when(core == 1)
    def _():
        rk_sibling(1).start()

    rk_ring(1).wait_recv()
    rk_sibling(0).wait_recv()
    for a in range(2):
        lr_left[a] = stand(rk_left[a])
    n_row, l_col = iota((2 * SLOTS, 128), 0), iota((2 * SLOTS, 128), 1)
    m_back[...] = hot(
        (l_col < 96) & (l_col // 48 == n_row // SLOTS) & ((l_col % 48) // 16 == (n_row % SLOTS) // CR) & (l_col % 16 == n_row % 16)
    )

    def own_tile(a, qa, qb):
        tile(
            left[a, qa].reshape(CR, D), lr_left[a, qa], own[qb].reshape(CR, D), lanes(rk_own, qb),
            (acc_left.at[a, 0, qa], acc_left.at[a, 1, qa]), (acc_right.at[0, 0, qb], acc_right.at[0, 1, qb]),
        )

    def far_tile(a, qa, qb):
        tile(
            left[a, qa].reshape(CR, D), lr_left[a, qa], right[qb].reshape(CR, D), lanes(rk_right, qb),
            (acc_left.at[a, 0, qa], acc_left.at[a, 1, qa]), (acc_right.at[1, 0, qb], acc_right.at[1, 1, qb]),
        )

    def arrived(way, q):
        straight(way, q).wait_recv()
        for d, detour in enumerate(DETOURS):
            if detour[0] == way:
                leg2(d, q).wait_recv()

    for q in range(CH):
        arrived(0, q)

        @pl.when(core == 1)
        def _():
            to_sibling(q, 1).start()

        to_sibling(q, 0).wait_recv()
        each(0, 2 * CH, lambda i: own_tile(i // CH, q, i % CH))
        arrived(1, q)
        each(0, 2 * (q + 1), lambda i: far_tile(i // (q + 1), q, i % (q + 1)))
        if q:
            each(0, 2 * q, lambda i: far_tile(i // q, i % q, q))

    def back1(i):
        t = (n + i) % PLANE
        return copy(b1s.at[t], b1r.at[s], ssb1.at[i], rsb1.at[i], plane_dev(t))

    def back2(i):
        g = (me + i) % COL
        return copy(b2s.at[g], b2r.at[me], ssb2.at[i], rsb2.at[i], col_dev(g))

    def lie(acc):
        return jnp.max(acc.reshape(SLOTS, 128).T, axis=0, keepdims=True)

    def flat(acc):
        return jnp.concatenate([jnp.max(acc[q], axis=0, keepdims=True) for q in range(CH)], axis=1)

    found = [[lie(acc_left[a, el]) for el in range(2)] for a in range(2)]
    found += [[flat(acc_right[r, el]) for el in range(2)] for r in range(2)]
    found = [jnp.concatenate([jnp.where(of_chip, m, 0.0) for m in f], axis=1) for f in found]
    found = pick(jnp.concatenate(found, axis=0), m_back[...], 3)
    for t in range(PLANE):
        for k in range(4):
            b1s[t, k : k + 1] = found[k * PLANE + t : k * PLANE + t + 1]
    each(1, PLANE, lambda i: back1(i).start())
    b1r[s] = b1s[n]
    a, b = iota((128, 256), 0), iota((128, 256), 1)
    unfold = hot((a // 48 == b // 128) & ((a % 48) // 16 == (b % 128) // 32) & (a % 2 == b % 2) & (b % 128 < 96))
    each(1, PLANE, lambda i: back1(i).wait_recv())

    def of(k):
        return jnp.concatenate([b1r[t, k : k + 1] for t in range(PLANE)], axis=0)

    def above(m):
        return jnp.concatenate([m[1:], m[:1]], axis=0)

    def below(m):
        return jnp.concatenate([m[PLANE - 1 :], m[: PLANE - 1]], axis=0)

    left0, left1, right0, right1 = of(0), above(of(1)), of(2), below(of(3))
    even = jnp.where(core == 0, jnp.maximum(jnp.maximum(right0, above(left0)), right1), left0)
    uneven = jnp.where(core == 0, left1, jnp.maximum(jnp.maximum(right0, left1), right1))
    wide = jnp.stack([even, uneven])[:, None]
    shape = (2, COL, PLANE, 128)
    wide = jnp.where((iota(shape, 3) % 16) // 2 == iota(shape, 1), wide, 0.0)
    wide = pick(wide.reshape(2 * COL * PLANE, 128), unfold, 3).reshape(2, COL, PLANE, 256)
    shape = (2, COL, PLANE, 256)
    wide = jnp.sum(jnp.where((iota(shape, 3) % 32) // 2 == iota(shape, 2), wide, 0.0), axis=2)
    wide = jnp.concatenate([wide[0], wide[1]], axis=1)
    for g in range(COL):
        b2s[g] = wide[g : g + 1]
    each(1, COL, lambda i: back2(i).start())
    b2r[me] = b2s[me]
    each(1, COL, lambda i: back2(i).wait_recv())
    got = jnp.concatenate([b2r[g] for g in range(COL)], axis=0)
    got = jnp.maximum(got[:4], got[4:])
    got = jnp.concatenate([got[:, c : c + 128] for c in (0, 256, 128, 384)], axis=0)
    got = pick(got, at_back, 3)
    out_early[...] = jnp.sum(jnp.where(at_goal, got[:COL], 0.0), axis=0)
    out_late[...] = jnp.sum(jnp.where(at_goal, got[COL:], 0.0), axis=0)

    each(1, COL, lambda i: rk1(i).wait_send())
    each(1, PLANE, lambda i: rk2(i).wait_send())
    for q in range(CH):
        each(1, COL, lambda i: row1a(q, i).wait_send())
        each(1, PLANE, lambda i: row2a(q, i).wait_send())
        each(1, PLANE, lambda i: row1b(q, i).wait_send())
        each(1, COL, lambda i: row2b(q, i).wait_send())
        straight(0, q).wait_send()
        straight(1, q).wait_send()
        for d in range(len(DETOURS)):
            leg1(d, q).wait_send()
            leg2(d, q).wait_send()
        to_sibling(q, 0).wait_send()
    rk_ring(0).wait_send()
    rk_ring(1).wait_send()
    rk_sibling(0).wait_send()
    each(1, PLANE, lambda i: back1(i).wait_send())
    each(1, COL, lambda i: back2(i).wait_send())


def body(embeddings, ranks, routes):
    dma = pltpu.SemaphoreType.DMA
    vm = pltpu.VMEM
    here = pl.BlockSpec(memory_space=vm)
    return tuple(pl.pallas_call(
        kernel,
        out_shape=[jax.ShapeDtypeStruct((ROWS,), F32)] * 2,
        in_specs=[pl.BlockSpec(memory_space=pltpu.HBM), here, here],
        out_specs=[here] * 2,
        scratch_shapes=[
            vm((ROWS, D), F32),
            vm((CH, COL, 32, HALF), BF16),
            vm((CH, COL, 32, HALF), BF16),
            vm((CH, PLANE, 16, HALF), BF16),
            vm((CH, PLANE, 16, HALF), BF16),
            vm((CH, PLANE, 16, HALF), BF16),
            vm((CH, COL, 32, HALF), BF16),
            vm((CH, COL, 32, HALF), BF16),
            vm((CH, PLANE, 16, D), BF16),
            vm((2, CH, PLANE, 16, D), BF16),
            vm((CH, PLANE, 16, D), BF16),
            vm((4, CH, 3, 16, D), BF16),
            vm((COL, 1, 128), F32),
            vm((COL, 1, 128), F32),
            vm((PLANE, 1, 128), F32),
            vm((PLANE, 1, 128), F32),
            vm((1, SLOTS), F32),
            vm((2, 1, SLOTS), F32),
            vm((1, SLOTS), F32),
            vm((CH, CR, 128), F32),
            vm((2, CH, CR, 128), F32),
            vm((2, 2, CH, CR, 128), F32),
            vm((2, 2, CH, 8, CR), F32),
            vm((PLANE, 4, 128), F32),
            vm((PLANE, 4, 128), F32),
            vm((COL, 1, 512), F32),
            vm((COL, 1, 512), F32),
            vm((128, SLOTS), BF16),
            vm((2 * SLOTS, 128), BF16),
            dma((CH, COL)), dma((CH, COL)),
            dma((CH, PLANE)), dma((CH, PLANE)),
            dma((CH, PLANE)), dma((CH, PLANE)),
            dma((CH, COL)), dma((CH, COL)),
            dma((COL,)), dma((COL,)),
            dma((PLANE,)), dma((PLANE,)),
            dma((3, CH)), dma((3, CH)),
            dma((4, CH)), dma((4, CH)),
            dma((4, CH)), dma((4, CH)),
            dma((3,)), dma((3,)),
            dma((PLANE,)), dma((PLANE,)),
            dma((COL,)), dma((COL,)),
            dma((4, CH)), dma,
        ],
        compiler_params=pltpu.CompilerParams(
            collective_id=0, has_side_effects=True, vmem_limit_bytes=48 * 2**20
        ),
    )(embeddings, ranks, routes.reshape(ROWS)))


def solution(mesh):
    placed = (P(("group", "blk"), None), P(("group", "blk")), P(("group", "blk"), None))
    return jax.shard_map(
        body,
        mesh=mesh,
        in_specs=placed,
        out_specs=(P(("group", "blk")), P(("group", "blk"))),
        check_vma=False,
    )
```

time: 97.2 us -> 84.1 us (0.87)
  Pallas kernels: 92.4 us -> 79.3 us
  other arithmetic: 1.88 us -> 0.7 us
  local copies, waits for them, and re-layouts: 2.09 us -> 3.24 us
    pallas_call x1, Pallas kernels: 92.4 us -> 79.3 us  [body(): pl.pallas_call(kernel, out_shape=[jax.ShapeDtypeStruct((ROWS,), F32)] * 2...]
    unnamed x2 -> x6, local copies, waits for them, and re-layouts: 1.41 us -> 3.24 us
    pallas_call x2 -> x0, other arithmetic: 1.19 us -> none  [body(): pl.pallas_call(kernel, out_shape=[jax.ShapeDtypeStruct((1, ROWS), F32)] *...]
where the time goes in v2:
time: 84.1 us; the launch traced here: 83.9 us
  Pallas kernels  79.3 us (94%)
  local copies, waits for them, and re-layouts  3.24 us (4%)
    pallas_call x1, Pallas kernels, body(): pl.pallas_call(kernel, out_shape=[jax.ShapeDtypeStruct((ROWS,), F32)] * 2...  79.3 us
    unnamed x6, local copies, waits for them, and re-layouts  3.24 us

profile of v2, /device:TPU:1, one launch (start us, length us, event | category | flops | bytes accessed | tf_op | source)
XLA Modules:
  0.0 83.9 jit_solution(1808214456676869164)
XLA Ops:
  0.6 0.7 reduce.routes
  1.3 0.0 copy-start
  1.3 1.4 %copy-done = f32[384,1024]{1,0:T(8,128)S(1)} copy-done((f32[384,1024]{1,0:T(8,128)S(1)}, f32[384,1024]{1,0:T(8,128)}, u32[]{:S(2)}) %copy-start) | copy-done | bytes 1572888
  2.7 0.0 copy-start.1
  2.7 0.7 copy-done.1
  3.4 79.3 %shard_map.50 = (f32[384]{0:T(512)S(1)}, f32[384]{0:T(512)S(1)}) custom-call(f32[384,1024]{1,0:T(8,128)S(1)} %copy-done, s32[384]{0:T(512)S(1)} %copy-done.1, s32[384]{0:T(512)S(1)} %reduce.routes), custom_call_target="tpu_custom_call" | custom-call | tf_op jit(solution)/shard_map/pallas_call | solution.py:481
  82.7 0.6 copy.7
  83.3 0.6 copy.8
Async XLA Ops:
  1.3 1.4 %copy-start = (f32[384,1024]{1,0:T(8,128)S(1)}, f32[384,1024]{1,0:T(8,128)}, u32[]{:S(2)}) copy-start(f32[384,1024]{1,0:T(8,128)} %emb_hbm.1) | copy-start | bytes 4718596
  2.7 0.7 copy-start.1

commit v3 on v2

v3 whole, which is shorter than its diff:
```python
import jax
import jax.numpy as jnp
from jax import lax
from jax.experimental import pallas as pl
from jax.experimental.pallas import tpu as pltpu
from jax.sharding import PartitionSpec as P

MESH = pl.DeviceIdType.MESH
F32 = jnp.float32
BF16 = jnp.bfloat16

D = 1024
VMEM_LIMIT = 62 * 2**20
HALF = 512
ROWS = 384
SLOTS = 768
CH = 3
CR = 256
COL = 8
PLANE = 16

RINGS = (
    (0, 4, 8, 12, 13, 1, 5, 9, 10, 14, 2, 6, 7, 11, 15, 3),
    (0, 1, 2, 3, 7, 4, 5, 6, 10, 11, 8, 9, 13, 14, 15, 12),
)
PLACES = tuple(tuple(r.index(n) for n in range(PLANE)) for r in RINGS)
UPS = tuple(tuple(r[(r.index(n) + 1) % PLANE] for n in range(PLANE)) for r in RINGS)
DOWNS = tuple(tuple(r[(r.index(n) - 1) % PLANE] for n in range(PLANE)) for r in RINGS)
STRAIGHT = 11
DETOURS = ((0, 1, 11, 14), (0, -1, 14, 16), (1, -1, 11, 14), (1, 1, 14, 16))


def iota(shape, dim):
    return lax.broadcasted_iota(jnp.int32, shape, dim)


def hot(mask):
    return jnp.where(mask, 1.0, 0.0).astype(BF16)


def pick(x, onehot, parts):
    rows = x.shape[0]
    pieces = []
    for _ in range(parts):
        piece = x.astype(BF16)
        pieces.append(piece)
        x = x - piece.astype(F32)
    out = jnp.dot(jnp.concatenate(pieces, axis=0), onehot, preferred_element_type=F32)
    total = out[(parts - 1) * rows :]
    for p in range(parts - 2, -1, -1):
        total = total + out[p * rows : (p + 1) * rows]
    return total


def look(tables, odd, index):
    found = index * 0
    for i in range(PLANE):
        found = jnp.where(index == i, jnp.where(odd == 1, tables[1][i], tables[0][i]), found)
    return found


def rem(a, b):
    return lax.rem(a, b)


def device(n, z, core):
    x, y = lax.div(n, 4), rem(n, 4)
    return (rem(y, 2) * 2 + core, lax.div(y, 2) * 16 + x * 4 + z)


def each(first, last, act):
    def step(i, c):
        act(i)
        return c

    lax.fori_loop(first, last, step, 0)


def kernel(
    emb_hbm, ranks_hbm, routes_hbm, out_early, out_late,
    emb, ranks, routes, send1a, recv1a, send2a, send1b, recv1b, send2b, recv2b, own, left, right, relay,
    rk1s, rk1r, rk2s, rk2r, rk_own, rk_left, rk_right,
    lr_own, lr_left, acc_left, acc_right,
    b1s, b1r, b2s, b2r, by_chip, by_goal, m_home, m_back, unfold,
    ss_row, rs1a, rs2a, rs1b, rs2b, ss_rank, rs_rank,
    ss_ring, rs_ring, ss_leg1, rs_leg1, ss_leg2, ss_back, rs_back, loc, in_sem,
):
    loads = [
        pltpu.make_async_copy(src, dst, in_sem.at[i])
        for i, (src, dst) in enumerate(((routes_hbm, routes), (ranks_hbm, ranks), (emb_hbm, emb)))
    ]
    for load in loads:
        load.start()
    grp = lax.axis_index("group")
    blk = lax.axis_index("blk")
    z, core = rem(blk, 4), rem(grp, 2)
    n = rem(lax.div(blk, 4), 4) * 4 + lax.div(blk, 16) * 2 + lax.div(grp, 2)
    me = core * 4 + z
    odd = rem(z, 2)

    def col_dev(g):
        return device(n, rem(g, 4), lax.div(g, 4))

    def plane_dev(t):
        return device(t, z, core)

    sibling = device(n, z, 1 - core)

    barrier = pltpu.get_barrier_semaphore()

    def greet(to):
        pl.semaphore_signal(barrier, inc=1, device_id=to, device_id_type=MESH)

    each(1, PLANE, lambda i: greet(plane_dev(rem(n + i, PLANE))))
    each(1, COL, lambda i: greet(col_dev(rem(me + i, COL))))
    s = look(PLACES, odd, n)
    up, down = look(UPS, odd, n), look(DOWNS, odd, n)
    beside = (look(UPS, 1 - odd, n), look(DOWNS, 1 - odd, n))
    for way, side, _, _ in DETOURS:
        greet(device(down if way == 0 else up, rem(z + 4 + side, 4), core))

    loads[0].wait()
    loads[1].wait()
    target = routes[...].reshape(1, ROWS)
    rank = ranks[...].reshape(1, ROWS).astype(F32) + 1.0
    spread = iota((128, ROWS), 0) == target
    before = hot(iota((ROWS, ROWS), 0) < iota((ROWS, ROWS), 1))
    count = jnp.dot(hot(spread), before, preferred_element_type=F32)
    slot = jnp.sum(jnp.where(spread, count, 0.0), axis=0, keepdims=True).astype(jnp.int32)
    cluster, block = target >> 5, target & 31
    goal = (block & 1) * 4 + cluster
    ring = block >> 1
    to_chip = look(RINGS, cluster & 1, ring)
    chunk, two = slot >> 1, slot & 1
    at_goal = iota((COL, ROWS), 0) == goal
    at_spot = hot(iota((128, ROWS), 0) == chunk * 32 + to_chip * 2 + two)
    at_back = hot(iota((128, ROWS), 0) == chunk * 32 + ring * 2 + two)
    ranks16 = jnp.concatenate([jnp.where(at_goal, rank, 0.0), jnp.zeros((COL, ROWS), F32)], axis=0)
    hi = ranks16.astype(BF16)
    lo = (ranks16 - hi.astype(F32)).astype(BF16)
    dims = (((1,), (1,)), ((), ()))
    packed = lax.dot_general(hi, at_spot, dims, preferred_element_type=F32) + lax.dot_general(
        lo, at_spot, dims, preferred_element_type=F32
    )
    for g in range(COL):
        rk1s[g] = packed[g : g + 1]
    loads[2].wait()
    e = emb[...]
    mean_square = jnp.mean(e * e, axis=-1, keepdims=True)
    unit = (e * lax.rsqrt(mean_square + 1e-06) * D ** (-0.5)).astype(BF16)

    def fill(q):
        for index, ref, first, shape in (
            (goal * 32 + to_chip * 2 + two, send1a, 0, (COL, 32, 256)),
            (to_chip * 16 + goal * 2 + two, send1b, HALF, (PLANE, 16, 256)),
        ):
            select = hot(iota((CR, ROWS), 0) == jnp.where(chunk == q, index, -1))
            for c in range(0, HALF, 256):
                rows = jnp.dot(select, unit[:, first + c : first + c + 256], preferred_element_type=F32)
                ref[q, :, :, c : c + 256] = rows.astype(BF16).reshape(shape)

    def copy(src, dst, send, recv, to):
        return pltpu.make_async_remote_copy(
            src_ref=src, dst_ref=dst, send_sem=send, recv_sem=recv, device_id=to, device_id_type=MESH
        )

    def rk1(i):
        g = rem(me + i, COL)
        return copy(rk1s.at[g], rk1r.at[me], ss_rank.at[0], rs_rank.at[0], col_dev(g))

    def rk2(i):
        t = rem(n + i, PLANE)
        return copy(rk2s.at[t], rk2r.at[n], ss_rank.at[1], rs_rank.at[1], plane_dev(t))

    def row1a(q, i):
        g = rem(me + i, COL)
        return copy(send1a.at[q, g], recv1a.at[q, me], ss_row.at[0], rs1a.at[q], col_dev(g))

    def row2a(q, i):
        t = rem(n + i, PLANE)
        return copy(send2a.at[q, t], own.at[q, n, :, pl.ds(0, HALF)], ss_row.at[1], rs2a.at[q], plane_dev(t))

    def row1b(q, i):
        t = rem(n + i, PLANE)
        return copy(send1b.at[q, t], recv1b.at[q, n], ss_row.at[2], rs1b.at[q], plane_dev(t))

    def row2b(q, i):
        g = rem(me + i, COL)
        return copy(send2b.at[q, g], recv2b.at[q, me], ss_row.at[3], rs2b.at[q], col_dev(g))

    def got_all(ref, sem):
        copy(ref, ref, ss_row.at[0], sem, sibling).wait_recv()

    def sent_all(ref, sem):
        copy(ref, ref, sem, rs_rank.at[0], sibling).wait_send()

    def stay1a(q):
        return pltpu.make_async_copy(send1a.at[q, me], recv1a.at[q, me], loc.at[0, q])

    def stay2a(q):
        return pltpu.make_async_copy(send2a.at[q, n], own.at[q, n, :, pl.ds(0, HALF)], loc.at[1, q])

    def stay1b(q):
        return pltpu.make_async_copy(send1b.at[q, n], recv1b.at[q, n], loc.at[2, q])

    def stay2b(q):
        return pltpu.make_async_copy(send2b.at[q, me], recv2b.at[q, me], loc.at[3, q])

    for q in range(CH):
        fill(q)

    a, b = iota((CR, CR), 0), iota((CR, CR), 1)
    by_chip[...] = hot(b == ((a & 15) >> 1) * 32 + (a >> 4) * 2 + (a & 1))
    by_goal[...] = hot(b == ((a & 31) >> 1) * 16 + (a >> 5) * 2 + (a & 1))
    lane = iota((128, SLOTS), 1)
    m_home[...] = hot(iota((128, SLOTS), 0) == (lane >> 8) * 16 + (lane & 15))
    lane = iota((CR, 128), 1)
    same = (lane & 15) == (iota((CR, 128), 0) & 15)
    for i in range(2 * CH):
        m_back[i * CR : (i + 1) * CR] = hot(same & (lane >> 4 == i))
    a, b = iota((128, 256), 0), iota((128, 256), 1)
    unfold[...] = hot(
        (a >> 4 == (b >> 7) * 3 + ((b & 127) >> 5)) & ((a & 1) == (b & 1)) & ((b & 127) < 96)
    )
    acc_left[...] = jnp.full(acc_left.shape, -1.0, F32)
    acc_right[...] = jnp.full(acc_right.shape, -1.0, F32)
    of_chip = ((iota((PLANE, SLOTS), 1) & 255) >> 4) == iota((PLANE, SLOTS), 0)

    pl.semaphore_wait(barrier, COL - 1 + PLANE - 1 + len(DETOURS))
    each(1, COL, lambda i: rk1(i).start())
    for q in range(CH):
        each(1, COL, lambda i: row1a(q, i).start())
        each(1, PLANE, lambda i: row1b(q, i).start())
        stay1a(q).start()
        stay1b(q).start()

    rk1r[me] = rk1s[me]
    got_all(rk1r.at[pl.ds(0, COL - 1)], rs_rank.at[0])
    seen = jnp.concatenate([rk1r[g] for g in range(COL)], axis=0)
    lane = iota((PLANE, COL, 128), 2)
    wide = jnp.where(((lane & 31) >> 1) == iota((PLANE, COL, 128), 0), seen[None], 0.0)
    a, b = iota((128, 128), 0), iota((128, 128), 1)
    fold = hot((a >> 5 == b >> 4) & ((a & 1) == (b & 1)) & (a < 96))
    wide = pick(wide.reshape(128, 128), fold, 2).reshape(PLANE, COL, 128)
    wide = jnp.sum(jnp.where(((lane & 15) >> 1) == iota((PLANE, COL, 128), 1), wide, 0.0), axis=1)
    for t in range(PLANE):
        rk2s[t] = wide[t : t + 1]
    each(1, PLANE, lambda i: rk2(i).start())
    rk2r[n] = rk2s[n]

    def turn(order, src, dst, q, first, shape):
        for c in range(0, HALF, 256):
            rows = jnp.dot(order[...], src[q, :, :, c : c + 256].reshape(CR, 256), preferred_element_type=F32)
            dst[q, :, :, first + c : first + c + 256] = rows.astype(BF16).reshape(shape)

    def regroup(q):
        got_all(recv1a.at[q, pl.ds(0, COL - 1)], rs1a.at[q])
        stay1a(q).wait()
        turn(by_chip, recv1a, send2a, q, 0, (PLANE, 16, 256))
        each(1, PLANE, lambda i: row2a(q, i).start())
        stay2a(q).start()
        got_all(recv1b.at[q, pl.ds(0, PLANE - 1)], rs1b.at[q])
        stay1b(q).wait()
        turn(by_goal, recv1b, send2b, q, 0, (COL, 32, 256))
        each(1, COL, lambda i: row2b(q, i).start())
        stay2b(q).start()

    def straight(way, q):
        rows = pl.ds(0, STRAIGHT)
        return copy(
            own.at[q, rows], left.at[core, q, rows] if way == 0 else right.at[q, rows],
            ss_ring.at[way], rs_ring.at[way, q], plane_dev(up if way == 0 else down),
        )

    def leg1(d, q):
        _, side, first, last = DETOURS[d]
        return copy(
            own.at[q, pl.ds(first, last - first)], relay.at[d, q, pl.ds(0, last - first)],
            ss_leg1.at[d], rs_leg1.at[d, q], device(n, rem(z + 4 + side, 4), core),
        )

    def leg2(d, q):
        way, side, first, last = DETOURS[d]
        rows = pl.ds(first, last - first)
        return copy(
            relay.at[d, q, pl.ds(0, last - first)], left.at[core, q, rows] if way == 0 else right.at[q, rows],
            ss_leg2.at[d], rs_ring.at[way, q], device(beside[way], rem(z + 4 - side, 4), core),
        )

    def to_sibling(q, k):
        return copy(own.at[q] if k == 0 else left.at[1, q], left.at[k, q], ss_ring.at[2], rs_ring.at[2, q], sibling)

    def rk_ring(way):
        return copy(
            rk_own, rk_left.at[core] if way == 0 else rk_right,
            ss_rank.at[2 + way], rs_rank.at[2 + way], plane_dev(up if way == 0 else down),
        )

    def rk_sibling(k):
        return copy(rk_own if k == 0 else rk_left.at[1], rk_left.at[k], ss_rank.at[4], rs_rank.at[4], sibling)

    def spread_out(q):
        got_all(recv2b.at[q, pl.ds(0, COL - 1)], rs2b.at[q])
        stay2b(q).wait()
        turn(by_chip, recv2b, own, q, HALF, (PLANE, 16, 256))
        got_all(own.at[q, pl.ds(0, PLANE - 1), :, pl.ds(0, HALF)], rs2a.at[q])
        stay2a(q).wait()
        for d in range(len(DETOURS)):
            leg1(d, q).start()
        straight(0, q).start()
        straight(1, q).start()

        @pl.when(core == 0)
        def _():
            to_sibling(q, 0).start()

    def pass_on(q):
        for d in range(len(DETOURS)):
            leg1(d, q).wait_recv()
            leg2(d, q).start()

    regroup(0)

    got_all(rk2r.at[pl.ds(0, PLANE - 1)], rs_rank.at[1])
    got = jnp.concatenate([rk2r[t] for t in range(PLANE)], axis=0)
    got = pick(got, m_home[...], 2)
    got = jnp.sum(jnp.where(of_chip, got, 0.0), axis=0, keepdims=True)
    rk_own[...] = jnp.where(got > 0.0, got, jnp.nan)
    rk_ring(0).start()
    rk_ring(1).start()

    @pl.when(core == 0)
    def _():
        rk_sibling(0).start()

    regroup(1)
    spread_out(0)
    regroup(2)
    spread_out(1)
    pass_on(0)
    spread_out(2)
    pass_on(1)

    def stand(row):
        return jnp.broadcast_to(row, (128, SLOTS)).T.reshape(CH, CR, 128)

    lr_own[...] = stand(rk_own[...])

    def compare(rows, lr, other, rr, accs_left, accs_right):
        scores = lax.dot_general(
            jnp.concatenate(rows, axis=0), other, dims, preferred_element_type=F32
        )
        lefts = [[None, None] for _ in rows]
        for h in range(0, other.shape[0], 128):
            rank_right = rr[:, h : h + 128]
            rights = [None, None]
            for i, lr_i in enumerate(lr):
                part = scores[i * CR : (i + 1) * CR, h : h + 128]
                low = jnp.where(rank_right < lr_i, part, -1.0)
                high = jnp.where(rank_right > lr_i, part, -1.0)
                for el, new in enumerate((low, high)):
                    if accs_left is not None:
                        lefts[i][el] = new if lefts[i][el] is None else jnp.maximum(lefts[i][el], new)
                    new = jnp.max(new.reshape(32, 8, 128), axis=0)
                    rights[1 - el] = new if rights[1 - el] is None else jnp.maximum(rights[1 - el], new)
            for el in range(2):
                accs_right[el][:, h : h + 128] = jnp.maximum(accs_right[el][:, h : h + 128], rights[el])
        if accs_left is not None:
            for acc, new in zip(accs_left, lefts, strict=True):
                for el in range(2):
                    acc[el][...] = jnp.maximum(acc[el][...], new[el])

    compare(
        [own[q].reshape(CR, D) for q in range(CH)], [lr_own[q] for q in range(CH)], own[...].reshape(SLOTS, D), rk_own[...],
        None, [acc_right.at[0, el] for el in range(2)],
    )
    pass_on(2)

    rk_ring(0).wait_recv()

    @pl.when(core == 1)
    def _():
        rk_sibling(1).start()

    rk_ring(1).wait_recv()
    rk_sibling(0).wait_recv()
    for a in range(2):
        lr_left[a] = stand(rk_left[a])

    def compare_left(parts, side, first, last):
        other, rr = (own, rk_own) if side == 0 else (right, rk_right)
        cols = pl.ds(first * CR, (last - first) * CR)
        compare(
            [left[a, q].reshape(CR, D) for a, q in parts], [lr_left[a, q] for a, q in parts],
            other[first:last].reshape((last - first) * CR, D), rr[:, first * CR : last * CR],
            [[acc_left.at[a, el, q] for el in range(2)] for a, q in parts],
            [acc_right.at[side, el, :, cols] for el in range(2)],
        )

    for q in range(CH):
        got_all(left.at[core, q], rs_ring.at[0, q])

        @pl.when(core == 1)
        def _():
            to_sibling(q, 1).start()

        got_all(left.at[1 - core, q], rs_ring.at[2, q])
        now = [(0, q), (1, q)]
        compare_left(now, 0, 0, CH)
        got_all(right.at[q], rs_ring.at[1, q])
        compare_left(now, 1, 0, q + 1)
        if q:
            compare_left([(a, p) for a in range(2) for p in range(q)], 1, q, q + 1)
        if q == 0:
            sent_all(send1a.at[:, pl.ds(0, COL - 1)], ss_row.at[0])
            sent_all(send2a.at[:, pl.ds(0, PLANE - 1)], ss_row.at[1])
            sent_all(send1b.at[:, pl.ds(0, PLANE - 1)], ss_row.at[2])
            sent_all(send2b.at[:, pl.ds(0, COL - 1)], ss_row.at[3])
            sent_all(rk1s.at[pl.ds(0, COL - 1)], ss_rank.at[0])
            sent_all(rk2s.at[pl.ds(0, PLANE - 1)], ss_rank.at[1])
            rk_ring(0).wait_send()
            rk_ring(1).wait_send()
            rk_sibling(0).wait_send()

    def back1(i):
        t = rem(n + i, PLANE)
        return copy(b1s.at[t], b1r.at[s], ss_back.at[0], rs_back.at[0], plane_dev(t))

    def back2(i):
        g = rem(me + i, COL)
        return copy(b2s.at[g], b2r.at[me], ss_back.at[1], rs_back.at[1], col_dev(g))

    def lie(acc):
        return jnp.max(acc.reshape(SLOTS, 128).T, axis=0, keepdims=True)

    def flat(acc):
        return jnp.max(acc, axis=0, keepdims=True)

    found = [[lie(acc_left[a, el]) for el in range(2)] for a in range(2)]
    found += [[flat(acc_right[r, el]) for el in range(2)] for r in range(2)]
    found = [jnp.concatenate([jnp.where(of_chip, m, 0.0) for m in f], axis=1) for f in found]
    found = pick(jnp.concatenate(found, axis=0), m_back[...], 3)
    for t in range(PLANE):
        for k in range(4):
            b1s[t, k : k + 1] = found[k * PLANE + t : k * PLANE + t + 1]
    each(1, PLANE, lambda i: back1(i).start())
    b1r[s] = b1s[n]
    got_all(b1r.at[pl.ds(0, PLANE - 1)], rs_back.at[0])

    def of(k):
        return jnp.concatenate([b1r[t, k : k + 1] for t in range(PLANE)], axis=0)

    def above(m):
        return jnp.concatenate([m[1:], m[:1]], axis=0)

    def below(m):
        return jnp.concatenate([m[PLANE - 1 :], m[: PLANE - 1]], axis=0)

    left0, left1, right0, right1 = of(0), above(of(1)), of(2), below(of(3))
    even = jnp.where(core == 0, jnp.maximum(jnp.maximum(right0, above(left0)), right1), left0)
    uneven = jnp.where(core == 0, left1, jnp.maximum(jnp.maximum(right0, left1), right1))
    wide = jnp.stack([even, uneven])[:, None]
    shape = (2, COL, PLANE, 128)
    wide = jnp.where(((iota(shape, 3) & 15) >> 1) == iota(shape, 1), wide, 0.0)
    wide = pick(wide.reshape(2 * COL * PLANE, 128), unfold[...], 3).reshape(2, COL, PLANE, 256)
    shape = (2, COL, PLANE, 256)
    wide = jnp.sum(jnp.where(((iota(shape, 3) & 31) >> 1) == iota(shape, 2), wide, 0.0), axis=2)
    wide = jnp.concatenate([wide[0], wide[1]], axis=1)
    for g in range(COL):
        b2s[g] = wide[g : g + 1]
    each(1, COL, lambda i: back2(i).start())
    b2r[me] = b2s[me]
    got_all(b2r.at[pl.ds(0, COL - 1)], rs_back.at[1])
    got = jnp.concatenate([b2r[g] for g in range(COL)], axis=0)
    got = jnp.maximum(got[:4], got[4:])
    got = jnp.concatenate([got[:, c : c + 128] for c in (0, 256, 128, 384)], axis=0)
    got = pick(got, at_back, 3)
    out_early[...] = jnp.sum(jnp.where(at_goal, got[:COL], 0.0), axis=0)
    out_late[...] = jnp.sum(jnp.where(at_goal, got[COL:], 0.0), axis=0)

    for way in range(2):
        sent_all(own.at[:, pl.ds(0, STRAIGHT)], ss_ring.at[way])
    sent_all(own, ss_ring.at[2])
    for d, (_, _, first, last) in enumerate(DETOURS):
        sent_all(own.at[:, pl.ds(first, last - first)], ss_leg1.at[d])
        sent_all(relay.at[d, :, pl.ds(0, last - first)], ss_leg2.at[d])
    sent_all(b1s.at[pl.ds(0, PLANE - 1)], ss_back.at[0])
    sent_all(b2s.at[pl.ds(0, COL - 1)], ss_back.at[1])


def body(embeddings, ranks, routes):
    dma = pltpu.SemaphoreType.DMA
    vm = pltpu.VMEM
    here = pl.BlockSpec(memory_space=vm)
    return tuple(pl.pallas_call(
        kernel,
        out_shape=[jax.ShapeDtypeStruct((ROWS,), F32)] * 2,
        in_specs=[pl.BlockSpec(memory_space=pltpu.HBM)] * 3,
        out_specs=[here] * 2,
        scratch_shapes=[
            vm((ROWS, D), F32),
            vm((ROWS,), jnp.int32),
            vm((1, ROWS), jnp.int32),
            vm((CH, COL, 32, HALF), BF16),
            vm((CH, COL, 32, HALF), BF16),
            vm((CH, PLANE, 16, HALF), BF16),
            vm((CH, PLANE, 16, HALF), BF16),
            vm((CH, PLANE, 16, HALF), BF16),
            vm((CH, COL, 32, HALF), BF16),
            vm((CH, COL, 32, HALF), BF16),
            vm((CH, PLANE, 16, D), BF16),
            vm((2, CH, PLANE, 16, D), BF16),
            vm((CH, PLANE, 16, D), BF16),
            vm((4, CH, 3, 16, D), BF16),
            vm((COL, 1, 128), F32),
            vm((COL, 1, 128), F32),
            vm((PLANE, 1, 128), F32),
            vm((PLANE, 1, 128), F32),
            vm((1, SLOTS), F32),
            vm((2, 1, SLOTS), F32),
            vm((1, SLOTS), F32),
            vm((CH, CR, 128), F32),
            vm((2, CH, CR, 128), F32),
            vm((2, 2, CH, CR, 128), F32),
            vm((2, 2, 8, SLOTS), F32),
            vm((PLANE, 4, 128), F32),
            vm((PLANE, 4, 128), F32),
            vm((COL, 1, 512), F32),
            vm((COL, 1, 512), F32),
            vm((CR, CR), BF16),
            vm((CR, CR), BF16),
            vm((128, SLOTS), BF16),
            vm((2 * SLOTS, 128), BF16),
            vm((128, 256), BF16),
            dma((4,)), dma((CH,)), dma((CH,)), dma((CH,)), dma((CH,)),
            dma((5,)), dma((5,)),
            dma((3,)), dma((3, CH)),
            dma((4,)), dma((4, CH)), dma((4,)),
            dma((2,)), dma((2,)),
            dma((4, CH)), dma((3,)),
        ],
        compiler_params=pltpu.CompilerParams(
            collective_id=0, has_side_effects=True, vmem_limit_bytes=VMEM_LIMIT
        ),
    )(embeddings, ranks, routes.reshape(1, ROWS)))


def solution(mesh):
    placed = (P(("group", "blk"), None), P(("group", "blk")), P(("group", "blk"), None))
    return jax.shard_map(
        body,
        mesh=mesh,
        in_specs=placed,
        out_specs=(P(("group", "blk")), P(("group", "blk"))),
        check_vma=False,
    )
```

time: 84.1 us -> 72.1 us (0.86)
  Pallas kernels: 79.3 us -> 68.8 us
    pallas_call x1, Pallas kernels: 79.3 us -> 68.8 us  [body(): pl.pallas_call(kernel, out_shape=[jax.ShapeDtypeStruct((ROWS,), F32)] * 2...]
    unnamed x6 -> x2, local copies, waits for them, and re-layouts: 3.24 us -> 2.48 us
where the time goes in v3:
time: 72.1 us; the launch traced here: 71.9 us
  Pallas kernels  68.8 us (95%)
  local copies, waits for them, and re-layouts  2.48 us (3%)
    pallas_call x1, Pallas kernels, body(): pl.pallas_call(kernel, out_shape=[jax.ShapeDtypeStruct((ROWS,), F32)] * 2...  68.8 us
    unnamed x2, local copies, waits for them, and re-layouts  2.48 us

profile of v3, /device:TPU:1, one launch (start us, length us, event | category | flops | bytes accessed | tf_op | source)
XLA Modules:
  0.0 71.9 jit_solution(6119569612561884481)
XLA Ops:
  0.6 68.8 %shard_map.50 = (f32[384]{0:T(512)}, f32[384]{0:T(512)}) custom-call(f32[384,1024]{1,0:T(8,128)} %emb_hbm.1, s32[384]{0:T(512)} %ranks_hbm.1, s32[1,384]{1,0:T(1,128)} %bitcast.1), custom_call_target="tpu_custom_call" | custom-call | tf_op jit(solution)/shard_map/pallas_call | solution.py:495
  69.4 1.2 %copy.7 = f32[384]{0:T(512)} copy(f32[384]{0:T(512)} %get-tuple-element.4) | data formatting | bytes 3072
  70.7 1.2 %copy.8 = f32[384]{0:T(512)} copy(f32[384]{0:T(512)} %get-tuple-element.5) | data formatting | bytes 3072

commit v4 on v3

--- a/solution.py
+++ b/solution.py
@@ -26,8 +26,14 @@
 PLACES = tuple(tuple(r.index(n) for n in range(PLANE)) for r in RINGS)
 UPS = tuple(tuple(r[(r.index(n) + 1) % PLANE] for n in range(PLANE)) for r in RINGS)
 DOWNS = tuple(tuple(r[(r.index(n) - 1) % PLANE] for n in range(PLANE)) for r in RINGS)
-STRAIGHT = 11
-DETOURS = ((0, 1, 11, 14), (0, -1, 14, 16), (1, -1, 11, 14), (1, 1, 14, 16))
+STRAIGHT = (12, 11, 12)
+DETOURS = ((0, 1, 0), (0, -1, 1), (1, -1, 0), (1, 1, 1))
+
+
+def span(share, q):
+    first = STRAIGHT[q]
+    middle = first + (PLANE - first + 1) // 2
+    return (first, middle) if share == 0 else (middle, PLANE)
 
 
 def iota(shape, dim):
@@ -77,7 +83,7 @@
 
 
 def kernel(
-    emb_hbm, ranks_hbm, routes_hbm, out_early, out_late,
+    emb_hbm, ranks_hbm, routes_hbm, out,
     emb, ranks, routes, send1a, recv1a, send2a, send1b, recv1b, send2b, recv2b, own, left, right, relay,
     rk1s, rk1r, rk2s, rk2r, rk_own, rk_left, rk_right,
     lr_own, lr_left, acc_left, acc_right,
@@ -116,7 +122,7 @@
     s = look(PLACES, odd, n)
     up, down = look(UPS, odd, n), look(DOWNS, odd, n)
     beside = (look(UPS, 1 - odd, n), look(DOWNS, 1 - odd, n))
-    for way, side, _, _ in DETOURS:
+    for way, side, _ in DETOURS:
         greet(device(down if way == 0 else up, rem(z + 4 + side, 4), core))
 
     loads[0].wait()
@@ -254,41 +260,43 @@
             dst[q, :, :, first + c : first + c + 256] = rows.astype(BF16).reshape(shape)
 
     def regroup(q):
+        got_all(recv1b.at[q, pl.ds(0, PLANE - 1)], rs1b.at[q])
+        stay1b(q).wait()
+        turn(by_goal, recv1b, send2b, q, 0, (COL, 32, 256))
+        each(1, COL, lambda i: row2b(q, i).start())
+        stay2b(q).start()
         got_all(recv1a.at[q, pl.ds(0, COL - 1)], rs1a.at[q])
         stay1a(q).wait()
         turn(by_chip, recv1a, send2a, q, 0, (PLANE, 16, 256))
         each(1, PLANE, lambda i: row2a(q, i).start())
         stay2a(q).start()
-        got_all(recv1b.at[q, pl.ds(0, PLANE - 1)], rs1b.at[q])
-        stay1b(q).wait()
-        turn(by_goal, recv1b, send2b, q, 0, (COL, 32, 256))
-        each(1, COL, lambda i: row2b(q, i).start())
-        stay2b(q).start()
 
     def straight(way, q):
-        rows = pl.ds(0, STRAIGHT)
+        rows = pl.ds(0, STRAIGHT[q])
         return copy(
             own.at[q, rows], left.at[core, q, rows] if way == 0 else right.at[q, rows],
-            ss_ring.at[way], rs_ring.at[way, q], plane_dev(up if way == 0 else down),
+            ss_ring.at[way, q], rs_ring.at[way, q], plane_dev(up if way == 0 else down),
         )
 
     def leg1(d, q):
-        _, side, first, last = DETOURS[d]
+        _, side, share = DETOURS[d]
+        first, last = span(share, q)
         return copy(
             own.at[q, pl.ds(first, last - first)], relay.at[d, q, pl.ds(0, last - first)],
-            ss_leg1.at[d], rs_leg1.at[d, q], device(n, rem(z + 4 + side, 4), core),
+            ss_leg1.at[d, q], rs_leg1.at[d, q], device(n, rem(z + 4 + side, 4), core),
         )
 
     def leg2(d, q):
-        way, side, first, last = DETOURS[d]
+        way, side, share = DETOURS[d]
+        first, last = span(share, q)
         rows = pl.ds(first, last - first)
         return copy(
             relay.at[d, q, pl.ds(0, last - first)], left.at[core, q, rows] if way == 0 else right.at[q, rows],
-            ss_leg2.at[d], rs_ring.at[way, q], device(beside[way], rem(z + 4 - side, 4), core),
+            ss_leg2.at[d, q], rs_ring.at[way, q], device(beside[way], rem(z + 4 - side, 4), core),
         )
 
     def to_sibling(q, k):
-        return copy(own.at[q] if k == 0 else left.at[1, q], left.at[k, q], ss_ring.at[2], rs_ring.at[2, q], sibling)
+        return copy(own.at[q] if k == 0 else left.at[1, q], left.at[k, q], ss_ring.at[2, q], rs_ring.at[2, q], sibling)
 
     def rk_ring(way):
         return copy(
@@ -475,15 +483,17 @@
     got = jnp.maximum(got[:4], got[4:])
     got = jnp.concatenate([got[:, c : c + 128] for c in (0, 256, 128, 384)], axis=0)
     got = pick(got, at_back, 3)
-    out_early[...] = jnp.sum(jnp.where(at_goal, got[:COL], 0.0), axis=0)
-    out_late[...] = jnp.sum(jnp.where(at_goal, got[COL:], 0.0), axis=0)
-
-    for way in range(2):
-        sent_all(own.at[:, pl.ds(0, STRAIGHT)], ss_ring.at[way])
-    sent_all(own, ss_ring.at[2])
-    for d, (_, _, first, last) in enumerate(DETOURS):
-        sent_all(own.at[:, pl.ds(first, last - first)], ss_leg1.at[d])
-        sent_all(relay.at[d, :, pl.ds(0, last - first)], ss_leg2.at[d])
+    out[0:1] = jnp.sum(jnp.where(at_goal, got[:COL], 0.0), axis=0, keepdims=True)
+    out[1:2] = jnp.sum(jnp.where(at_goal, got[COL:], 0.0), axis=0, keepdims=True)
+
+    for q in range(CH):
+        for way in range(2):
+            sent_all(own.at[q, pl.ds(0, STRAIGHT[q])], ss_ring.at[way, q])
+        sent_all(own.at[q], ss_ring.at[2, q])
+        for d, (_, _, share) in enumerate(DETOURS):
+            first, last = span(share, q)
+            sent_all(own.at[q, pl.ds(first, last - first)], ss_leg1.at[d, q])
+            sent_all(relay.at[d, q, pl.ds(0, last - first)], ss_leg2.at[d, q])
     sent_all(b1s.at[pl.ds(0, PLANE - 1)], ss_back.at[0])
     sent_all(b2s.at[pl.ds(0, COL - 1)], ss_back.at[1])
 
@@ -492,11 +502,11 @@
     dma = pltpu.SemaphoreType.DMA
     vm = pltpu.VMEM
     here = pl.BlockSpec(memory_space=vm)
-    return tuple(pl.pallas_call(
+    out = pl.pallas_call(
         kernel,
-        out_shape=[jax.ShapeDtypeStruct((ROWS,), F32)] * 2,
+        out_shape=jax.ShapeDtypeStruct((2, ROWS), F32),
         in_specs=[pl.BlockSpec(memory_space=pltpu.HBM)] * 3,
-        out_specs=[here] * 2,
+        out_specs=here,
         scratch_shapes=[
             vm((ROWS, D), F32),
             vm((ROWS,), jnp.int32),
@@ -511,7 +521,7 @@
             vm((CH, PLANE, 16, D), BF16),
             vm((2, CH, PLANE, 16, D), BF16),
             vm((CH, PLANE, 16, D), BF16),
-            vm((4, CH, 3, 16, D), BF16),
+            vm((4, CH, 4, 16, D), BF16),
             vm((COL, 1, 128), F32),
             vm((COL, 1, 128), F32),
             vm((PLANE, 1, 128), F32),
@@ -534,15 +544,16 @@
             vm((128, 256), BF16),
             dma((4,)), dma((CH,)), dma((CH,)), dma((CH,)), dma((CH,)),
             dma((5,)), dma((5,)),
-            dma((3,)), dma((3, CH)),
-            dma((4,)), dma((4, CH)), dma((4,)),
+            dma((3, CH)), dma((3, CH)),
+            dma((4, CH)), dma((4, CH)), dma((4, CH)),
             dma((2,)), dma((2,)),
             dma((4, CH)), dma((3,)),
         ],
         compiler_params=pltpu.CompilerParams(
             collective_id=0, has_side_effects=True, vmem_limit_bytes=VMEM_LIMIT
         ),
-    )(embeddings, ranks, routes.reshape(1, ROWS)))
+    )(embeddings, ranks, routes.reshape(1, ROWS))
+    return out[0], out[1]
 
 
 def solution(mesh):

time: 72.1 us -> 70.4 us (0.976)
  local copies, waits for them, and re-layouts: 2.48 us -> 1.36 us
    unnamed x2 -> x0, local copies, waits for them, and re-layouts: 2.48 us -> none
    slice x0 -> x1, local copies, waits for them, and re-layouts: none -> 1.36 us  [body(): return (out[0], out[1])]
where the time goes in v4:
time: 70.4 us; the launch traced here: 70.3 us
  Pallas kernels  68.3 us (97%)
  local copies, waits for them, and re-layouts  1.36 us (2%)
    pallas_call x1, Pallas kernels, body(): pl.pallas_call(kernel, out_shape=jax.ShapeDtypeStruct((2, ROWS), F32), in...  68.3 us

profile of v4, /device:TPU:1, one launch (start us, length us, event | category | flops | bytes accessed | tf_op | source)
XLA Modules:
  0.0 70.3 jit_solution(10845086221989728460)
XLA Ops:
  0.6 68.3 %shard_map.50 = f32[2,384]{1,0:T(2,128)} custom-call(f32[384,1024]{1,0:T(8,128)} %emb_hbm.1, s32[384]{0:T(512)} %ranks_hbm.1, s32[1,384]{1,0:T(1,128)} %bitcast.1), custom_call_target="tpu_custom_call" | custom-call | tf_op jit(solution)/shard_map/pallas_call | solution.py:505
  68.9 1.4 %slice_reduce_fusion = (f32[384]{0:T(512)}, f32[384]{0:T(512)}) fusion(f32[2,384]{1,0:T(2,128)} %shard_map.50), kind=kLoop, calls=%fused_computation | loop fusion | bytes 6144 | tf_op jit(solution)/shard_map/slice | solution.py:556

commit v5 on v4

--- a/solution.py
+++ b/solution.py
@@ -26,7 +26,7 @@
 PLACES = tuple(tuple(r.index(n) for n in range(PLANE)) for r in RINGS)
 UPS = tuple(tuple(r[(r.index(n) + 1) % PLANE] for n in range(PLANE)) for r in RINGS)
 DOWNS = tuple(tuple(r[(r.index(n) - 1) % PLANE] for n in range(PLANE)) for r in RINGS)
-STRAIGHT = (12, 11, 12)
+STRAIGHT = (11, 12, 11)
 DETOURS = ((0, 1, 0), (0, -1, 1), (1, -1, 0), (1, 1, 1))
 
 
@@ -34,6 +34,9 @@
     first = STRAIGHT[q]
     middle = first + (PLANE - first + 1) // 2
     return (first, middle) if share == 0 else (middle, PLANE)
+
+
+MIXED = (10, 1, 4, 3, 12, 2, 8, 5, 15, 7, 13, 6, 9, 14, 11)
 
 
 def iota(shape, dim):
@@ -75,11 +78,8 @@
 
 
 def each(first, last, act):
-    def step(i, c):
+    for i in range(first, last):
         act(i)
-        return c
-
-    lax.fori_loop(first, last, step, 0)
 
 
 def kernel(
@@ -117,13 +117,9 @@
     def greet(to):
         pl.semaphore_signal(barrier, inc=1, device_id=to, device_id_type=MESH)
 
-    each(1, PLANE, lambda i: greet(plane_dev(rem(n + i, PLANE))))
+    for i in MIXED:
+        greet(plane_dev(rem(n + i, PLANE)))
     each(1, COL, lambda i: greet(col_dev(rem(me + i, COL))))
-    s = look(PLACES, odd, n)
-    up, down = look(UPS, odd, n), look(DOWNS, odd, n)
-    beside = (look(UPS, 1 - odd, n), look(DOWNS, 1 - odd, n))
-    for way, side, _ in DETOURS:
-        greet(device(down if way == 0 else up, rem(z + 4 + side, 4), core))
 
     loads[0].wait()
     loads[1].wait()
@@ -215,6 +211,10 @@
     for q in range(CH):
         fill(q)
 
+    s = look(PLACES, odd, n)
+    up, down = look(UPS, odd, n), look(DOWNS, odd, n)
+    beside = (look(UPS, 1 - odd, n), look(DOWNS, 1 - odd, n))
+
     a, b = iota((CR, CR), 0), iota((CR, CR), 1)
     by_chip[...] = hot(b == ((a & 15) >> 1) * 32 + (a >> 4) * 2 + (a & 1))
     by_goal[...] = hot(b == ((a & 31) >> 1) * 16 + (a >> 5) * 2 + (a & 1))
@@ -232,11 +232,13 @@
     acc_right[...] = jnp.full(acc_right.shape, -1.0, F32)
     of_chip = ((iota((PLANE, SLOTS), 1) & 255) >> 4) == iota((PLANE, SLOTS), 0)
 
-    pl.semaphore_wait(barrier, COL - 1 + PLANE - 1 + len(DETOURS))
+    pl.semaphore_wait(barrier, COL - 1 + PLANE - 1)
     each(1, COL, lambda i: rk1(i).start())
     for q in range(CH):
-        each(1, COL, lambda i: row1a(q, i).start())
-        each(1, PLANE, lambda i: row1b(q, i).start())
+        for i, t in enumerate(MIXED):
+            row1b(q, t).start()
+            if i % 2 == 0 and i // 2 + 1 < COL:
+                row1a(q, i // 2 + 1).start()
         stay1a(q).start()
         stay1b(q).start()
 
@@ -268,7 +270,8 @@
         got_all(recv1a.at[q, pl.ds(0, COL - 1)], rs1a.at[q])
         stay1a(q).wait()
         turn(by_chip, recv1a, send2a, q, 0, (PLANE, 16, 256))
-        each(1, PLANE, lambda i: row2a(q, i).start())
+        for i in MIXED:
+            row2a(q, i).start()
         stay2a(q).start()
 
     def straight(way, q):

time: 70.4 us -> 69.5 us (0.987)
  Pallas kernels: 68.3 us -> 67.4 us
    pallas_call x1, Pallas kernels: 68.3 us -> 67.4 us  [body(): pl.pallas_call(kernel, out_shape=jax.ShapeDtypeStruct((2, ROWS), F32), in...]
where the time goes in v5:
time: 69.5 us; the launch traced here: 69.4 us
  Pallas kernels  67.4 us (97%)
  local copies, waits for them, and re-layouts  1.36 us (2%)
    pallas_call x1, Pallas kernels, body(): pl.pallas_call(kernel, out_shape=jax.ShapeDtypeStruct((2, ROWS), F32), in...  67.4 us

profile of v5, /device:TPU:1, one launch (start us, length us, event | category | flops | bytes accessed | tf_op | source)
XLA Modules:
  0.0 69.4 jit_solution(6776364089921319632)
XLA Ops:
  0.6 67.4 %shard_map.50 = f32[2,384]{1,0:T(2,128)} custom-call(f32[384,1024]{1,0:T(8,128)} %emb_hbm.1, s32[384]{0:T(512)} %ranks_hbm.1, s32[1,384]{1,0:T(1,128)} %bitcast.1), custom_call_target="tpu_custom_call" | custom-call | tf_op jit(solution)/shard_map/pallas_call | solution.py:508
  68.0 1.4 %slice_reduce_fusion = (f32[384]{0:T(512)}, f32[384]{0:T(512)}) fusion(f32[2,384]{1,0:T(2,128)} %shard_map.50), kind=kLoop, calls=%fused_computation | loop fusion | bytes 6144 | tf_op jit(solution)/shard_map/slice | solution.py:559

commit v6 on v5

--- a/solution.py
+++ b/solution.py
@@ -415,9 +415,14 @@
         def _():
             to_sibling(q, 1).start()
 
-        got_all(left.at[1 - core, q], rs_ring.at[2, q])
         now = [(0, q), (1, q)]
-        compare_left(now, 0, 0, CH)
+        if q < CH - 1:
+            got_all(left.at[1 - core, q], rs_ring.at[2, q])
+            compare_left(now, 0, 0, CH)
+        else:
+            compare_left([(core, q)], 0, 0, CH)
+            got_all(left.at[1 - core, q], rs_ring.at[2, q])
+            compare_left([(1 - core, q)], 0, 0, CH)
         got_all(right.at[q], rs_ring.at[1, q])
         compare_left(now, 1, 0, q + 1)
         if q:

time: 69.5 us -> 69.2 us (level)
  no operation moved by 1% of the time
where the time goes in v6:
time: 69.2 us; the launch traced here: 69 us
  Pallas kernels  67 us (97%)
  local copies, waits for them, and re-layouts  1.36 us (2%)
    pallas_call x1, Pallas kernels, body(): pl.pallas_call(kernel, out_shape=jax.ShapeDtypeStruct((2, ROWS), F32), in...  67 us

profile of v6, /device:TPU:1, one launch (start us, length us, event | category | flops | bytes accessed | tf_op | source)
XLA Modules:
  0.0 69.0 jit_solution(173593239844670403)
XLA Ops:
  0.6 67.0 %shard_map.50 = f32[2,384]{1,0:T(2,128)} custom-call(f32[384,1024]{1,0:T(8,128)} %emb_hbm.1, s32[384]{0:T(512)} %ranks_hbm.1, s32[1,384]{1,0:T(1,128)} %bitcast.1), custom_call_target="tpu_custom_call" | custom-call | tf_op jit(solution)/shard_map/pallas_call | solution.py:513
  67.7 1.4 %slice_reduce_fusion = (f32[384]{0:T(512)}, f32[384]{0:T(512)}) fusion(f32[2,384]{1,0:T(2,128)} %shard_map.50), kind=kLoop, calls=%fused_computation | loop fusion | bytes 6144 | tf_op jit(solution)/shard_map/slice | solution.py:564
